TPU v7x, 32 devices: a whole 2x2x4 slice. The times are simulated.
32 devices in a mesh: groups: 2 (over y), xy: 4 (over z), gz: 2 (over x), sub: 2 (over core).
Axes of the slice: x: 2, y: 2, z: 4, core: 2. Of those that a mesh axis runs over, the one named last changes fastest.
Arguments:
- top_plane: bfloat16 [128, 256, 128], P(('groups', 'xy'), ('sub', 'gz')), parts along dimension 0, may hold values from -6 to 6
- front_plane: bfloat16 [128, 32, 128], P(('groups', 'xy'), 'gz', 'sub'), parts along dimension 0, may hold values from -6 to 6
- side_plane: bfloat16 [512, 32, 128], P(('groups', 'sub'), 'gz', 'xy'), parts along dimension 0, may hold values from -6 to 6
- labels: int32 [128, 32, 256], P(('groups', 'xy'), 'gz', 'sub'), parts along dimension 0, may hold values from 0 to 17
- w_in: bfloat16 [128, 128], replicated, may hold values from -0.5 to 0.5
- b_in: float32 [128], replicated, may hold values from -3 to 3
- w_out: bfloat16 [128, 18], replicated, may hold values from -1.5 to 1.5
- b_out: float32 [18], replicated, may hold values from -3 to 3
Outputs:
- grad_top: float32 [128, 256, 128], P(('groups', 'xy'), ('sub', 'gz')), parts along dimension 0
- grad_front: float32 [128, 32, 128], P(('groups', 'xy'), 'gz', 'sub'), parts along dimension 0
- grad_side: float32 [512, 32, 128], P(('groups', 'sub'), 'gz', 'xy'), parts along dimension 0
- grad_w_in: float32 [256, 128], P('groups'), parts along dimension 0
- grad_b_in: float32 [256], P('groups'), parts along dimension 0
- grad_w_out: float32 [256, 18], P('groups'), parts along dimension 0
- grad_b_out: float32 [36], P('groups'), parts along dimension 0
There are 2 independent parts, one for each index of `groups`. A program takes and returns all parts, laid end to end along the dimension named above; an argument that names none is the same for every part. Nothing has to cross between parts.
All inputs are finite; a program needn't handle non-finite values.
Results may differ from a plain program's by a relative error of at most 0.0026.
Values may be sent and summed in bfloat16 or wider, within the bound.
A program may use at most 64 MiB of HBM per device.

v0:
```python
import jax
import jax.numpy as jnp
from jax import lax
from jax.sharding import PartitionSpec as P


def on_device(top_plane, front_plane, side_plane, labels, w_in, b_in, w_out, b_out):
    front_full = lax.all_gather(front_plane, "sub", axis=2, tiled=True)
    side_full = lax.all_gather(side_plane, "xy", axis=2, tiled=True)
    top_full = lax.all_gather(top_plane, "gz", axis=1, tiled=True)
    rows_y, rows_z, chans = side_full.shape
    total = (
        labels.shape[0]
        * labels.shape[1]
        * labels.shape[2]
        * lax.axis_size("xy")
        * lax.axis_size("gz")
        * lax.axis_size("sub")
    )
    side_f = side_full.astype(jnp.float32)
    classes = jnp.arange(w_out.shape[1], dtype=jnp.int32)

    def step(carry, inputs):
        side_acc, gw1, gb1, gw2, gb2 = carry
        top_row, front_row, label_row = inputs
        feat = (
            (
                top_row[:, None, :].astype(jnp.float32)
                + front_row[None, :, :].astype(jnp.float32)
                + side_f
            )
            .astype(jnp.bfloat16)
            .reshape(rows_y * rows_z, chans)
        )
        pre = jnp.dot(feat, w_in, preferred_element_type=jnp.float32) + b_in
        sig = jax.nn.sigmoid(pre)
        hid = (pre * sig).astype(jnp.bfloat16)
        logits_t = (
            lax.dot_general(
                w_out, hid, (((0,), (1,)), ((), ())), preferred_element_type=jnp.float32
            )
            + b_out[:, None]
        )
        expo = jnp.exp(logits_t)
        prob = expo / jnp.sum(expo, axis=0, keepdims=True)
        onehot = (label_row.T.reshape(-1)[None, :] == classes[:, None]).astype(jnp.float32)
        dlog = (prob - onehot).astype(jnp.bfloat16)
        dhid = lax.dot_general(
            dlog, w_out, (((0,), (1,)), ((), ())), preferred_element_type=jnp.float32
        )
        dpre = (dhid * sig * (1.0 + pre * (1.0 - sig))).astype(jnp.bfloat16)
        dfeat = lax.dot_general(
            dpre, w_in, (((1,), (1,)), ((), ())), preferred_element_type=jnp.float32
        )
        gw1 = gw1 + lax.dot_general(
            feat, dpre, (((0,), (0,)), ((), ())), preferred_element_type=jnp.float32
        )
        gb1 = gb1 + jnp.sum(dpre.astype(jnp.float32), axis=0)
        gw2 = gw2 + lax.dot_general(
            hid, dlog, (((0,), (1,)), ((), ())), preferred_element_type=jnp.float32
        )
        gb2 = gb2 + jnp.sum(dlog.astype(jnp.float32), axis=1)
        dgrid = dfeat.reshape(rows_y, rows_z, chans)
        side_acc = side_acc + dgrid
        return ((side_acc, gw1, gb1, gw2, gb2), (jnp.sum(dgrid, axis=1), jnp.sum(dgrid, axis=0)))

    side_init = jnp.zeros((rows_y, rows_z, chans), jnp.float32)
    init = (
        side_init,
        jnp.zeros(w_in.shape, jnp.float32),
        jnp.zeros(b_in.shape, jnp.float32),
        jnp.zeros(w_out.shape, jnp.float32),
        jnp.zeros(b_out.shape, jnp.float32),
    )
    carry, outs = lax.scan(step, init, (top_full, front_full, labels))
    side_acc, gw1, gb1, gw2, gb2 = carry
    top_terms, front_terms = outs
    grad_top = lax.psum_scatter(top_terms, "gz", scatter_dimension=1, tiled=True)
    grad_front = lax.psum_scatter(front_terms, "sub", scatter_dimension=2, tiled=True)
    grad_side = lax.psum_scatter(side_acc, "xy", scatter_dimension=2, tiled=True)
    gw1, gb1, gw2, gb2 = lax.psum((gw1, gb1, gw2, gb2), ("xy", "gz", "sub"))
    return (grad_top, grad_front, grad_side, gw1 / total, gb1 / total, gw2 / total, gb2 / total)


def solution(mesh):
    in_specs = (
        P(("groups", "xy"), ("sub", "gz"), None),
        P(("groups", "xy"), "gz", "sub"),
        P(("groups", "sub"), "gz", "xy"),
        P(("groups", "xy"), "gz", "sub"),
        P(),
        P(),
        P(),
        P(),
    )
    out_specs = (
        P(("groups", "xy"), ("sub", "gz"), None),
        P(("groups", "xy"), "gz", "sub"),
        P(("groups", "sub"), "gz", "xy"),
        P("groups", None),
        P("groups"),
        P("groups", None),
        P("groups"),
    )
    return jax.shard_map(
        on_device, mesh=mesh, in_specs=in_specs, out_specs=out_specs, check_vma=False
    )
```

profile of v0, /device:TPU:0, one launch (start us, length us, event | category | flops | bytes accessed | tf_op | source)
XLA Modules:
  0.0 227.6 jit_solution(2676509718950982056)
XLA Ops:
  8.1 1.0 copy.21
  9.4 2.3 all_gather.10
  12.1 17.5 %all_gather.11 = bf16[128,16,128]{0,1,2:T(8,128)(2,1)S(1)} all-gather(bf16[128,16,32]{0,1,2:T(8,128)(2,1)S(1)} %copy.21), channel_id=1, replica_groups=mesh['groups'=2,'xy'=4,'gz'=2,'sub'=2] {'xy'}, dimensions={2}, use_global_device_ids=true | all-gather | bytes 655360 | tf_op jit(solution)/shard_map/all_gather | solution.py:9
  30.6 7.9 %all_gather.9 = bf16[16,128,128]{2,1,0:T(8,128)(2,1)} all-gather(bf16[16,64,128]{2,1,0:T(8,128)(2,1)S(1)} %copy-done.2), channel_id=1, replica_groups=mesh['groups'=2,'xy'=4,'gz'=2,'sub'=2] {'gz'}, dimensions={1}, use_global_device_ids=true | all-gather | bytes 786432 | tf_op jit(solution)/shard_map/all_gather | solution.py:10
  38.5 86.3 %while.23 = (s32[]{:T(128)}, f32[128,16,128]{2,1,0:T(8,128)S(1)}, f32[128,128]{1,0:T(8,128)S(1)}, f32[128]{0:T(128)S(1)}, f32[128,18]{0,1:T(8,128)S(1)}, /*index...) while((s32[]{:T(128)}, f32[128,16,128]{2,1,0:T(8,128)S(1)}, ...), condition=%wide.region_6.7_spmd.clone, body=%wide.region_0.6_spmd.clone.sunk | while | flops 236296848 | bytes 13281347 | solution.py:75
  39.4 0.8 bitcast_convert_fusion.5
  44.8 0.8 bitcast_convert_fusion.5
  50.2 0.8 bitcast_convert_fusion.5
  55.6 0.8 bitcast_convert_fusion.5
  60.9 0.8 bitcast_convert_fusion.5
  66.3 0.8 bitcast_convert_fusion.5
  77.1 0.8 bitcast_convert_fusion.5
  82.5 0.8 bitcast_convert_fusion.5
  87.9 0.8 bitcast_convert_fusion.5
  93.3 0.8 bitcast_convert_fusion.5
  98.7 0.8 bitcast_convert_fusion.5
  104.1 0.8 bitcast_convert_fusion.5
  125.9 1.1 reshape.45
  127.7 1.4 copy.25
  129.1 58.7 %all-reduce = (f32[128]{0:T(128)S(1)}, f32[128,18]{0,1:T(8,128)S(1)}, f32[18]{0:T(128)S(1)}) all-reduce(f32[128]{0:T(128)S(1)} %get-tuple-element.104, f32[128,18]{0,1:T(8,128)S(1)} %get-tuple-element.105, f32[18]{0:T(128)S(1)} %get-tuple-element.106), channel_id=1, replica_groups=mesh['groups'=2,'xy'=4,'gz'=2,'sub'=2] {'xy','gz','sub'}, use_global_device_ids=true, to_apply=%region_11.12 | all-reduce | flops 2450 | bytes 19600 | tf_op jit(solution)/shard_map/psum | solution.py:81
  189.5 27.1 %all-reduce.3.cloned.1.call-done = f32[128,128]{1,0:T(8,128)} async-done(((f32[128,128]{1,0:T(8,128)}), f32[128,128]{1,0:T(8,128)}) %all-reduce.3.cloned.1.call-update) | async-done | bytes 65552 | tf_op jit(solution)/shard_map/psum | solution.py:81
  216.6 1.5 broadcast_multiply_fusion
  218.0 1.0 reshape.46
  219.1 0.9 copy.27
  (315 shorter events, 81.2 us)
Async XLA Ops:
  8.0 208.6 %all-reduce.3.cloned.1.call-start = ((), (), s32[]{:S(2)}) async-start(), calls=%async_computation.5 | async-start | bytes 131072 | tf_op jit(solution)/shard_map/psum | solution.py:81
  8.1 1.0 copy-start.4
  29.6 1.0 copy-start.2
  30.5 7.9 %copy-start.1 = (bf16[128,128]{1,0:T(8,128)(2,1)S(1)}, bf16[128,128]{1,0:T(8,128)(2,1)}, u32[]{:S(2)}) copy-start(bf16[128,128]{1,0:T(8,128)(2,1)} %param.14) | copy-start | bytes 98308
  30.5 7.9 %copy-start.3 = (bf16[128,18]{0,1:T(8,128)(2,1)S(1)}, bf16[128,18]{0,1:T(8,128)(2,1)}, u32[]{:S(2)}) copy-start(bf16[128,18]{0,1:T(8,128)(2,1)} %param.16) | copy-start | bytes 13828
  30.5 7.9 %copy-start.5 = (f32[18]{0:T(128)S(1)}, f32[18]{0:T(128)}, u32[]{:S(2)}) copy-start(f32[18]{0:T(128)} %param.17) | copy-start | bytes 220
  30.6 7.9 %copy-start.6 = (f32[128]{0:T(128)S(1)}, f32[128]{0:T(128)}, u32[]{:S(2)}) copy-start(f32[128]{0:T(128)} %param.15) | copy-start | bytes 1540
  124.7 0.6 copy-start
  125.4 92.6 %reduce-scatter.10.cloned.1.call-start = ((), (), s32[]{:S(2)}) async-start(), calls=%async_computation.6 | async-start | bytes 196608
  127.0 93.0 %reduce-scatter.6.cloned.1.call-start = ((), (), s32[]{:S(2)}) async-start(), calls=%async_computation.3 | async-start | bytes 1572864 | tf_op jit(solution)/shard_map/reduce_scatter | solution.py:78
  127.6 92.4 %reduce-scatter.8.cloned.1.call-start = ((), (), s32[]{:S(2)}) async-start(), calls=%async_computation.4 | async-start | bytes 1310720 | tf_op jit(solution)/shard_map/reduce_scatter | solution.py:80
Sparse Core Ops, SparseCore 0:
  125.5 91.0 all-reduce.2
Sparse Core Ops, SparseCore 1:
  128.6 8.3 reduce-scatter.9
  139.6 21.8 reduce-scatter.5
  164.4 27.4 reduce-scatter.7
where the time goes:
time: 231 us; the launch traced here: 228 us
  blocking collectives  86.4 us (37%)
  matrix products  41.6 us (18%)
  local copies, waits for them, and re-layouts  32.4 us (14%)
  waiting for transfers between devices  27.6 us (12%)
  other arithmetic  22.5 us (10%)
  between operations  15.8 us (7%)
    psum x1, blocking collectives, on_device(): gw1, gb1, gw2, gb2 = lax.psum((gw1, gb1, gw2, gb2), ('xy', 'gz', 'sub'))  58.7 us
    psum x1, waiting for transfers between devices, on_device(): gw1, gb1, gw2, gb2 = lax.psum((gw1, gb1, gw2, gb2), ('xy', 'gz', 'sub'))  27.1 us
    all_gather x1, blocking collectives, on_device(): side_full = lax.all_gather(side_plane, 'xy', axis=2, tiled=True)  17.5 us
    dynamic_slice x32, local copies, waits for them, and re-layouts, on_device(): carry, outs = lax.scan(step, init, (top_full, front_full, labels))  12.8 us
    convert_element_type x16, other arithmetic, step(): top_row[:, None, :].astype(jnp.float32)  12.3 us
    dot_general x16, matrix products, step(): lax.dot_general(dpre, w_in, (((1,), (1,)), ((), ())), preferred_element_t...  10.3 us
    dynamic_update_slice x32, local copies, waits for them, and re-layouts, on_device(): carry, outs = lax.scan(step, init, (top_full, front_full, labels))  10.2 us
    dot_general x16, matrix products, step(): lax.dot_general(dlog, w_out, (((0,), (1,)), ((), ())), preferred_element_...  9.29 us
  transfers between devices with their start and end apart: 4, of which 1 were waited for; matrix products, arithmetic and copies ran while one was open for 4% of the time, Pallas kernels for 0%

commit v1 on v0

v1 whole, which is shorter than its diff:
```python
import functools

import jax
import jax.numpy as jnp
from jax import lax
from jax.experimental import pallas as pl
from jax.experimental.pallas import tpu as pltpu
from jax.sharding import PartitionSpec as P

F32 = jnp.float32
BF16 = jnp.bfloat16
KP = 32
KU = 24
L = 128


def dot(a, b, ca=1, cb=0):
    return lax.dot_general(a, b, (((ca,), (cb,)), ((), ())), preferred_element_type=F32)


def split(v):
    hi = v.astype(BF16)
    return hi, (v - hi.astype(F32)).astype(BF16)


def exact_dot(v, w, cb):
    hi, lo = split(v)
    return dot(hi, w, 1, cb) + dot(lo, w, 1, cb)


def kernel(cfg, top_ref, front_ref, side_ref, lab_ref, w_ref, b_ref, wo_ref, bo_ref,
           otop_ref, ofront_ref, oside_ref, ogw_ref,
           top_all, front_all, side_all, e_side, e_front, wp, t_s, f_s, s_s, hid_s, g_s,
           a_top, a_front, a_side, a_gw2, a_gb2,
           top_snd, top_rcv, front_snd, front_rcv, side_snd, side_rcv,
           gw_loc, gw_sub, gw_gz, gw_part2, gw_xy, gw_half,
           sem_s, sem_r):
    ns, nx, ng, nb_, nch, yc, xs, zs, total = cfg
    nsub = nb_
    ix, ig, isub = lax.axis_index("xy"), lax.axis_index("gz"), lax.axis_index("sub")
    ids = {"xy": (ix, nx), "gz": (ig, ng), "sub": (isub, nsub)}
    r = L // yc
    nblk = zs // r
    qs = ns
    zq = zs // qs
    cs = L // ns
    cf = L // nsub

    def peer(axis, s):
        me, n = ids[axis]
        return lax.rem(me + s, n)

    def source(axis, s):
        me, n = ids[axis]
        return lax.rem(me + n - s, n)

    counter = [0]

    def remote(src, dst, axis, s):
        k = counter[0]
        counter[0] += 1
        return pltpu.make_async_remote_copy(
            src_ref=src, dst_ref=dst, send_sem=sem_s.at[k], recv_sem=sem_r.at[k],
            device_id={axis: peer(axis, s)}, device_id_type=pl.DeviceIdType.MESH)

    bar = pltpu.get_barrier_semaphore()
    greet = 0
    for axis in ("sub", "gz", "xy"):
        for s in range(1, ids[axis][1]):
            pl.semaphore_signal(bar, inc=1, device_id={axis: peer(axis, s)}, device_id_type=pl.DeviceIdType.MESH)
            greet += 1
    pl.semaphore_wait(bar, greet)

    started = []

    def go(copy):
        copy.start()
        started.append(copy)
        return copy

    side_cp = [[go(remote(side_ref.at[c], side_all.at[s - 1, c], "xy", s)) for s in range(1, ns)] for c in range(1)]
    top_cp = [go(remote(top_ref, top_all.at[s - 1], "gz", s)) for s in range(1, ng)]
    front_cp = [go(remote(front_ref, front_all.at[s - 1], "sub", s)) for s in range(1, nsub)]
    side_cp += [[go(remote(side_ref.at[c], side_all.at[s - 1, c], "xy", s)) for s in range(1, ns)] for c in range(1, nch)]

    w = w_ref[...]
    e_side[...] = jnp.zeros_like(e_side)
    for j in range(ns):
        for q in range(qs):
            e_side[j, q * cs:(q + 1) * cs, q * L:(q + 1) * L] = w[j * cs:(j + 1) * cs, :]
    e_front[...] = jnp.zeros_like(e_front)
    for j in range(nsub):
        for q in range(nsub):
            e_front[j, q * cf:(q + 1) * cf, q * L:(q + 1) * L] = w[j * cf:(j + 1) * cf, :]
    wp[...] = jnp.zeros_like(wp)
    wp[0:KP, 0:L] = wo_ref[...]
    wp[KP:2 * KP, L:2 * L] = wo_ref[...]
    a_side[...] = jnp.zeros_like(a_side)
    a_front[...] = jnp.zeros_like(a_front)
    a_gw2[...] = jnp.zeros_like(a_gw2)
    a_gb2[...] = jnp.zeros_like(a_gb2)

    yb = top_ref.shape[1]

    def project_top(plane, owner):
        v = (dot(plane.reshape(xs * yb, L), w) + b_ref[...]) * 0.5
        t_s[:, pl.ds(pl.multiple_of(owner * yb, yb), yb), :] = v.reshape(xs, yb, L)

    project_top(top_ref[...], ig)
    for s in range(1, ng):
        top_cp[s - 1].wait_recv()
        project_top(top_all[s - 1], source("gz", s))

    for cp in front_cp:
        cp.wait_recv()
    fp = dot(front_ref[...], e_front[isub])
    for s in range(1, nsub):
        fp = fp + dot(front_all[s - 1], e_front[source("sub", s)])
    fp = fp * 0.5
    frows = xs * zs // nsub
    for q in range(nsub):
        f_s[q * (xs // nsub):(q + 1) * (xs // nsub)] = fp[:, q * L:(q + 1) * L].reshape(xs // nsub, zs, L)

    iota_k = lax.broadcasted_iota(jnp.int32, (KU, L), 0)
    bo = bo_ref[0:KU, :]
    out_cp = []

    for c in range(nch):
        for cp in side_cp[c]:
            cp.wait_recv()
        sp = dot(side_ref[c], e_side[ix if ns > 1 else 0])
        for s in range(1, ns):
            sp = sp + dot(side_all[s - 1, c], e_side[source("xy", s)])
        sp = sp * 0.5
        bq = nblk // qs
        for q in range(qs):
            s_s[q * bq:(q + 1) * bq] = sp[:, q * L:(q + 1) * L].reshape(bq, L, L)

        def x_body(xi, _):
            t_x = t_s[xi, c * yc:(c + 1) * yc, :]
            t_blk = jnp.concatenate([t_x] * r, axis=0) if r > 1 else t_x
            f_x = f_s[xi]
            top_acc = jnp.zeros((yc, L), F32)
            gw2 = jnp.zeros((KP, L), F32)
            gb2 = jnp.zeros((KU, L), F32)
            for pair in range(nblk // 2):
                hs = []
                for i in range(2):
                    b = pair * 2 + i
                    if r > 1:
                        f_blk = jnp.concatenate(
                            [jnp.broadcast_to(f_x[b * r + k:b * r + k + 1], (yc, L)) for k in range(r)], axis=0)
                    else:
                        f_blk = f_x[b:b + 1]
                    p = t_blk + (s_s[b] + f_blk)
                    t = jnp.tanh(p)
                    u = 1.0 + t
                    hid = p * u
                    g_s[b] = (u + hid * (1.0 - t)).astype(BF16)
                    hs.append(hid.astype(BF16))
                h_cat = jnp.concatenate(hs, axis=1)
                logits = dot(wp[...], h_cat, 1, 1)
                dls = []
                for i in range(2):
                    b = pair * 2 + i
                    lg = logits[i * KP:i * KP + KU] + bo
                    ex = jnp.exp(lg - jnp.max(lg, axis=0, keepdims=True))
                    prob = ex * (1.0 / jnp.sum(ex, axis=0, keepdims=True))
                    lab = lab_ref[xi, c, b:b + 1, :]
                    dl = prob - jnp.where(iota_k == lab, 1.0, 0.0)
                    gb2 = gb2 + dl
                    dls.append(jnp.concatenate([dl, jnp.zeros((KP - KU, L), F32)], axis=0).astype(BF16))
                gw2 = gw2 + dot(jnp.concatenate(dls, axis=1), jnp.concatenate(hs, axis=0))
                dhid = dot(jnp.concatenate(dls, axis=0), wp[...], 0, 0)
                for i in range(2):
                    b = pair * 2 + i
                    dpre = dhid[:, i * L:(i + 1) * L] * g_s[b].astype(F32)
                    a_side[c, b] += dpre
                    for k in range(r):
                        part = dpre[k * yc:(k + 1) * yc]
                        top_acc = top_acc + part
                        z = b * r + k
                        a_front[xi, z:z + 1, :] += jnp.sum(part, axis=0, keepdims=True)
            a_top[xi, c * yc:(c + 1) * yc, :] = top_acc
            a_gw2[...] += gw2
            a_gb2[...] += gb2
            return 0

        lax.fori_loop(0, xs, x_body, 0)

        acc = a_side[c] * 0.5
        a_side[c] = acc
        cat = jnp.concatenate([acc[q * bq:(q + 1) * bq].reshape(bq * L, L) for q in range(qs)], axis=1)
        hi, lo = split(cat)
        for s in range(1, ns):
            e = e_side[peer("xy", s)]
            side_snd[s - 1, c] = (dot(hi, e, 1, 1) + dot(lo, e, 1, 1)).astype(BF16)
            out_cp.append((c, s, go(remote(side_snd.at[s - 1, c], side_rcv.at[s - 1, c], "xy", s))))
        e = e_side[ix if ns > 1 else 0]
        oside_ref[c] = dot(hi, e, 1, 1) + dot(lo, e, 1, 1)

    a_top[...] = a_top[...] * 0.5
    front_sum = a_front[...] * 0.5
    gw1 = jnp.zeros((L, L), F32)
    for s in range(ng):
        plane = top_ref[...] if s == 0 else top_all[s - 1]
        own = ig if s == 0 else source("gz", s)
        rows = a_top[:, pl.ds(pl.multiple_of(own * yb, yb), yb), :].reshape(xs * yb, L)
        gw1 = gw1 + dot(plane.reshape(xs * yb, L), rows.astype(BF16), 0, 0)
        if s > 0:
            top_snd[s - 1] = exact_dot(rows, w, 1).astype(BF16).reshape(xs, yb, L)
    for s in range(1, ng):
        go_cp = go(remote(top_snd.at[ng - s - 1], top_rcv.at[s - 1], "gz", s))
        out_cp.append(("top", s, go_cp))

    fcat = jnp.concatenate(
        [front_sum[q * (xs // nsub):(q + 1) * (xs // nsub)].reshape(frows, L) for q in range(nsub)], axis=1)
    fhi, flo = split(fcat)
    for s in range(1, nsub):
        e = e_front[peer("sub", s)]
        front_snd[s - 1] = dot(fhi, e, 1, 1) + dot(flo, e, 1, 1)
        out_cp.append(("front", s, go(remote(front_snd.at[s - 1], front_rcv.at[s - 1], "sub", s))))
    e = e_front[isub]
    ofront_ref[...] = dot(fhi, e, 1, 1) + dot(flo, e, 1, 1)

    for s in range(nsub):
        plane = front_ref[...] if s == 0 else front_all[s - 1]
        own = isub if s == 0 else source("sub", s)
        m = dot(plane, fhi, 0, 0)
        v = jnp.zeros((cf, L), F32)
        for q in range(nsub):
            v = v + m[q * cf:(q + 1) * cf, q * L:(q + 1) * L]
        gw_loc[pl.ds(pl.multiple_of(own * cf, cf), cf), :] = v
    gw_loc[0:L, :] = gw_loc[0:L, :] + gw1
    for s in range(ns):
        own = (ix if s == 0 else source("xy", s)) if ns > 1 else 0
        v = jnp.zeros((cs, L), F32)
        for c in range(nch):
            plane = side_ref[c] if s == 0 else side_all[s - 1, c]
            cat = jnp.concatenate(
                [a_side[c, q * bq:(q + 1) * bq].reshape(bq * L, L).astype(BF16) for q in range(qs)], axis=1)
            m = dot(plane, cat, 0, 0)
            for q in range(qs):
                v = v + m[q * cs:(q + 1) * cs, q * L:(q + 1) * L]
        at = pl.ds(pl.multiple_of(own * cs, cs), cs)
        gw_loc[at, :] = gw_loc[at, :] + v
    gw_loc[L:L + KU, :] = a_gw2[0:KU, :]
    gb1 = jnp.sum(front_sum.reshape(xs * zs, L), axis=0, keepdims=True)
    gb2 = jnp.sum(a_gb2[...], axis=1, keepdims=True)
    eye = (lax.broadcasted_iota(jnp.int32, (KU, L), 0) == lax.broadcasted_iota(jnp.int32, (KU, L), 1)).astype(F32)
    gb2_row = jnp.sum(gb2 * eye, axis=0, keepdims=True)
    gw_loc[L + KU:L + KU + 8, :] = jnp.concatenate([gb1, gb2_row, jnp.zeros((6, L), F32)], axis=0)

    hr = (L + KU + 8) // nsub

    def rows_of(i):
        return pl.ds(pl.multiple_of(i * hr, hr), hr)

    cps = [go(remote(gw_loc.at[rows_of(peer("sub", s))], gw_sub.at[s - 1], "sub", s)) for s in range(1, nsub)]
    part = gw_loc[rows_of(isub), :]
    for s in range(1, nsub):
        cps[s - 1].wait_recv()
        part = part + gw_sub[s - 1]
    gw_gz[ig] = part
    cps = [go(remote(gw_gz.at[ig], gw_gz.at[ig], "gz", s)) for s in range(1, ng)]
    own_rows = a_top[:, pl.ds(pl.multiple_of(ig * yb, yb), yb), :].reshape(xs * yb, L)
    otop_ref[...] = exact_dot(own_rows, w, 1).reshape(xs, yb, L)
    for cp in cps:
        cp.wait_recv()
    part = gw_gz[0]
    for j in range(1, ng):
        part = part + gw_gz[j]
    gw_part2[ix] = part * (1.0 / total)
    cps = [go(remote(gw_part2.at[ix], gw_part2.at[ix], "xy", s)) for s in range(1, nx)]
    for cp in cps:
        cp.wait_recv()
    full = gw_part2[0]
    for j in range(1, nx):
        full = full + gw_part2[j]
    ogw_ref[rows_of(isub), :] = full
    gw_half[...] = full
    cps = [go(remote(gw_half, gw_xy.at[s - 1], "sub", s)) for s in range(1, nsub)]
    for s in range(1, nsub):
        cps[s - 1].wait_recv()
        ogw_ref[rows_of(source("sub", s)), :] = gw_xy[s - 1]

    for kind, s, cp in out_cp:
        cp.wait_recv()
        if kind == "top":
            otop_ref[...] += top_rcv[s - 1].astype(F32)
        elif kind == "front":
            ofront_ref[...] += front_rcv[s - 1]
        else:
            oside_ref[kind] += side_rcv[s - 1, kind].astype(F32)
    for cp in started:
        cp.wait_send()


NCH = 1


def on_device(nx, ng, nsub, top, front, side, labels, w_in, b_in, w_out, b_out):
    xs, zs, ys = labels.shape
    total = xs * zs * ys * nx * ng * nsub
    k = w_out.shape[1]
    ns = nx if L // nx >= 16 else 1
    if ns == 1:
        side = lax.all_gather(side, "xy", axis=2, tiled=True)
    nch = NCH
    yc = ys // nch
    r = L // yc
    cs, cf = L // ns, L // nsub
    zq = zs // ns
    side_p = side.reshape(nch, yc, ns, zq, cs).transpose(0, 3, 1, 2, 4).reshape(nch, zq * yc, L)
    front_p = front.reshape(nsub, xs * zs // nsub, cf).transpose(1, 0, 2).reshape(xs * zs // nsub, L)
    lab = labels.reshape(xs, zs // r, r, nch, yc).transpose(0, 3, 1, 2, 4).reshape(xs, nch, zs // r, L)
    wo = jnp.zeros((KP, L), BF16).at[:k].set(w_out.T)
    bo = jnp.full((KP, L), -1e30, F32).at[:k].set(jnp.broadcast_to(b_out[:, None], (k, L)))
    yb = top.shape[1]
    fr, sr = front_p.shape[0], zq * yc
    gr = L + KU + 8
    nblk = zs // r
    copies = nch * (ns - 1) * 2 + (ng - 1) * 3 + (nsub - 1) * 4 + (nx - 1)
    cfg = (ns, nx, ng, nsub, nch, yc, xs, zs, total)
    vm = pl.BlockSpec(memory_space=pltpu.VMEM)
    V = pltpu.VMEM
    one = max(ns - 1, 1)
    otop, ofront, oside, ogw = pl.pallas_call(
        functools.partial(kernel, cfg),
        out_shape=(
            jax.ShapeDtypeStruct(top.shape, F32),
            jax.ShapeDtypeStruct((fr, L), F32),
            jax.ShapeDtypeStruct((nch, sr, L), F32),
            jax.ShapeDtypeStruct((gr, L), F32),
        ),
        in_specs=[vm] * 8,
        out_specs=(vm,) * 4,
        scratch_shapes=[
            V((ng - 1,) + top.shape, BF16), V((nsub - 1, fr, L), BF16), V((one, nch, sr, L), BF16),
            V((ns, L, ns * L), BF16), V((nsub, L, nsub * L), BF16), V((2 * KP, 2 * L), BF16),
            V((xs, ys, L), F32), V((xs, zs, L), F32), V((nblk, L, L), F32),
            V((8, L), F32), V((nblk, L, L), BF16),
            V((xs, ys, L), F32), V((xs, zs, L), F32), V((nch, nblk, L, L), F32),
            V((KP, L), F32), V((KU, L), F32),
            V((ng - 1,) + top.shape, BF16), V((ng - 1,) + top.shape, BF16),
            V((nsub - 1, fr, L), F32), V((nsub - 1, fr, L), F32),
            V((one, nch, sr, L), BF16), V((one, nch, sr, L), BF16),
            V((gr, L), F32), V((nsub - 1, gr // nsub, L), F32),
            V((ng, gr // nsub, L), F32), V((nx, gr // nsub, L), F32),
            V((nsub - 1, gr // nsub, L), F32), V((gr // nsub, L), F32),
            pltpu.SemaphoreType.DMA((copies,)), pltpu.SemaphoreType.DMA((copies,)),
        ],
        compiler_params=pltpu.CompilerParams(
            collective_id=0, has_side_effects=True, vmem_limit_bytes=48 * 1024 * 1024),
    )(top, front_p, side_p, lab, w_in, b_in.reshape(1, L), wo, bo)
    gfront = ofront.reshape(fr, nsub, cf).transpose(1, 0, 2).reshape(front.shape)
    gside = oside.reshape(nch, zq, yc, ns, cs).transpose(0, 2, 3, 1, 4).reshape(side.shape)
    if ns == 1:
        gside = lax.psum_scatter(gside, "xy", scatter_dimension=2, tiled=True)
    return (otop, gfront, gside, ogw[:L], ogw[L + KU], ogw[L:L + k].T, ogw[L + KU + 1, :k])


def solution(mesh):
    in_specs = (
        P(("groups", "xy"), ("sub", "gz"), None),
        P(("groups", "xy"), "gz", "sub"),
        P(("groups", "sub"), "gz", "xy"),
        P(("groups", "xy"), "gz", "sub"),
        P(),
        P(),
        P(),
        P(),
    )
    out_specs = (
        P(("groups", "xy"), ("sub", "gz"), None),
        P(("groups", "xy"), "gz", "sub"),
        P(("groups", "sub"), "gz", "xy"),
        P("groups", None),
        P("groups"),
        P("groups", None),
        P("groups"),
    )
    body = functools.partial(on_device, mesh.shape["xy"], mesh.shape["gz"], mesh.shape["sub"])
    return jax.shard_map(body, mesh=mesh, in_specs=in_specs, out_specs=out_specs, check_vma=False)
```

time: 231 us -> 77.3 us (0.33); the launches traced: 228 us -> 77 us
  blocking collectives: 86.4 us -> 0 us
  Pallas kernels: 0 us -> 68.2 us
  matrix products: 41.6 us -> 0 us
  waiting for transfers between devices: 27.6 us -> 0 us
  local copies, waits for them, and re-layouts: 32.4 us -> 8.03 us
  other arithmetic: 22.5 us -> 0 us
  between operations: 15.8 us -> 0.75 us
    pallas_call x0 -> x1, Pallas kernels: none -> 68.2 us  [on_device(): pl.pallas_call(functools.partial(kernel, cfg), out_shape=(jax.ShapeDtypeS...]
    psum x1 -> x0, blocking collectives: 58.7 us -> none  [on_device(): gw1, gb1, gw2, gb2 = lax.psum((gw1, gb1, gw2, gb2), ('xy', 'gz', 'sub'))]
    dot_general x96 -> x0, matrix products: 41.6 us -> none  [the longest x16 10.3 us: step(): lax.dot_general(dpre, w_in, (((1,), (1,)), ((), ())), preferred_element_t...]
    all_gather x3 -> x0, blocking collectives: 27.7 us -> none  [the longest x1 17.5 us: on_device(): side_full = lax.all_gather(side_plane, 'xy', axis=2, tiled=True)]
    psum x1 -> x0, waiting for transfers between devices: 27.1 us -> none  [on_device(): gw1, gb1, gw2, gb2 = lax.psum((gw1, gb1, gw2, gb2), ('xy', 'gz', 'sub'))]
    convert_element_type x32 -> x0, other arithmetic: 14.2 us -> none  [the longest x16 12.3 us: step(): top_row[:, None, :].astype(jnp.float32)]
    dynamic_slice x32 -> x0, local copies, waits for them, and re-layouts: 12.8 us -> none  [on_device(): carry, outs = lax.scan(step, init, (top_full, front_full, labels))]
    dynamic_update_slice x32 -> x0, local copies, waits for them, and re-layouts: 10.2 us -> none  [on_device(): carry, outs = lax.scan(step, init, (top_full, front_full, labels))]
  transfers between devices with their start and end apart: 4 -> 0, of which waited for: 1 -> 0; matrix products, arithmetic and copies ran while one was open for 4% -> 0% of each run, Pallas kernels for 0% -> 0%
where the time goes in v1:
time: 77.3 us; the launch traced here: 77 us
  Pallas kernels  68.2 us (88%)
  local copies, waits for them, and re-layouts  8.03 us (10%)
    pallas_call x1, Pallas kernels, on_device(): pl.pallas_call(functools.partial(kernel, cfg), out_shape=(jax.ShapeDtypeS...  68.2 us
    unnamed x15, local copies, waits for them, and re-layouts  2.61 us

profile of v1, /device:TPU:0, one launch (start us, length us, event | category | flops | bytes accessed | tf_op | source)
XLA Modules:
  0.0 77.0 jit_solution(4197712926635651154)
XLA Ops:
  0.6 1.0 %copy.33 = bf16[1,128,4,4,32]{1,3,4,2,0:T(4,128)(2,1)S(1)} copy(bf16[1,128,4,4,32]{1,4,3,2,0:T(8,128)(2,1)} %bitcast.35) | data formatting | bytes 262144 | tf_op jit(solution)/shard_map/reshape | solution.py:314
  1.6 0.0 copy-start.4
  1.6 0.1 reshape.92
  1.7 0.0 copy-start
  1.7 0.1 copy.27.side_ref
  1.8 0.0 copy-start.1
  1.8 0.6 copy-done.4
  2.5 0.1 copy.24
  2.6 0.0 copy-start.6
  2.6 0.1 copy.26.front_ref
  2.7 0.5 copy-done.6
  3.2 0.1 scatter.14.bo_ref
  3.3 0.0 copy-start.3
  3.3 0.6 copy-done.2
  4.0 68.2 %shard_map.135 = (f32[16,64,128]{2,1,0:T(8,128)S(1)}, f32[128,128]{1,0:T(8,128)S(1)}, f32[1,512,128]{2,1,0:T(8,128)S(1)}, f32[160,128]{1,0:T(8,128)S(1)}) custom-call(bf16[16,64,128]{2,1,0:T(8,128)(2,1)S(1)} %copy-done, bf16[128,128]{1,0:T(8,128)(2,1)S(1)} %copy.26.front_ref, bf16[1,512,128]{2,1,0:T(8,128)(2,1)S(1)} %copy.27.side_ref, ...), custom_call_target="tpu_custom_call" | custom-call | tf_op jit(solution)/shard_map/pallas_call | solution.py:328
  72.2 0.6 slice.44
  72.8 0.6 slice_bitcast_fusion
  73.4 0.5 slice_bitcast_fusion.1
  73.9 0.5 slice_bitcast_fusion.2
  74.5 0.1 copy.30
  74.6 0.7 copy.31
  75.3 0.1 copy.28
  75.4 0.8 copy.29
  76.2 0.8 %copy.35 = f32[16,64,128]{2,1,0:T(8,128)} copy(f32[16,64,128]{2,1,0:T(8,128)S(1)} %get-tuple-element.46) | data formatting | bytes 1048576
  (8 shorter events, 0.0 us)
Async XLA Ops:
  1.6 0.8 %copy-start.4 = (bf16[16,16,64]{2,1,0:T(8,128)(2,1)S(1)}, bf16[16,16,64]{2,1,0:T(8,128)(2,1)}, u32[]{:S(2)}) copy-start(bf16[16,16,64]{2,1,0:T(8,128)(2,1)} %param.13) | copy-start | bytes 98308
  1.7 1.6 %copy-start = (bf16[16,64,128]{2,1,0:T(8,128)(2,1)S(1)}, bf16[16,64,128]{2,1,0:T(8,128)(2,1)}, u32[]{:S(2)}) copy-start(bf16[16,64,128]{2,1,0:T(8,128)(2,1)} %top_ref.1) | copy-start | bytes 786436
  1.8 1.5 %copy-start.1 = (s32[16,16,128]{2,1,0:T(8,128)S(1)}, s32[16,16,128]{2,1,0:T(8,128)}, u32[]{:S(2)}) copy-start(s32[16,16,128]{2,1,0:T(8,128)} %param.15) | copy-start | bytes 393220
  2.6 0.7 copy-start.6
  2.6 0.7 copy-start.5
  3.2 0.8 copy-start.2
  3.3 0.7 copy-start.3

commit v2 on v0

v2 whole, which is shorter than its diff:
```python
import functools

import jax
import jax.numpy as jnp
from jax import lax
from jax.experimental import pallas as pl
from jax.experimental.pallas import tpu as pltpu
from jax.sharding import PartitionSpec as P

F32 = jnp.float32
BF16 = jnp.bfloat16
KP = 32
KU = 24
L = 128
CHUNKS = 2


def dot(a, b, ca=1, cb=0):
    return lax.dot_general(a, b, (((ca,), (cb,)), ((), ())), preferred_element_type=F32)


def split(v):
    hi = v.astype(BF16)
    return hi, (v - hi.astype(F32)).astype(BF16)


def kernel(cfg, top_ref, front_ref, side_ref, lab_ref, w_ref, b_ref, wo_ref, bo_ref,
           otop_ref, ofront_ref, oside_ref, ogw1_ref, ogw2_ref, ogb_ref,
           top_all, front_all, side_all, wp, wl, ww, t_s, f_s, s_s, hid_s, g_s, dl_s, g_side,
           a_top, a_front, a_side, a_gw2, a_gb2,
           top_snd, top_rcv, front_snd, front_rcv, side_snd, side_rcv,
           gw_loc, gw_sub, gw_gz, gw_xy, gw_full,
           sem_s, sem_r):
    ns, nx, ng, nsub, xs, zs, ys, k, total = cfg
    ix, ig, isub = lax.axis_index("xy"), lax.axis_index("gz"), lax.axis_index("sub")
    ids = {"xy": (ix, nx), "gz": (ig, ng), "sub": (isub, nsub)}
    cs, cf = L // ns, L // nsub
    zc = zs // CHUNKS
    pairs = zc // 2
    yb = top_ref.shape[1]

    def peer(axis, s):
        me, n = ids[axis]
        return lax.rem(me + s, n)

    def source(axis, s):
        me, n = ids[axis]
        return lax.rem(me + n - s, n)

    counter = [0]
    started = []

    def go(src, dst, axis, s):
        i = counter[0]
        counter[0] += 1
        copy = pltpu.make_async_remote_copy(
            src_ref=src, dst_ref=dst, send_sem=sem_s.at[i], recv_sem=sem_r.at[i],
            device_id={axis: peer(axis, s)}, device_id_type=pl.DeviceIdType.MESH)
        copy.start()
        started.append(copy)
        return copy

    bar = pltpu.get_barrier_semaphore()
    greet = 0
    for axis in ("sub", "gz", "xy"):
        for s in range(1, ids[axis][1]):
            pl.semaphore_signal(bar, inc=1, device_id={axis: peer(axis, s)}, device_id_type=pl.DeviceIdType.MESH)
            greet += 1
    pl.semaphore_wait(bar, greet)

    def channels(i):
        return pl.ds(pl.multiple_of(i * cs, cs), cs)

    def columns(i):
        return pl.ds(pl.multiple_of(i * cf, cf), cf)

    def rows_y(i):
        return pl.ds(pl.multiple_of(i * yb, yb), yb)

    def heights(c):
        return pl.ds(c * zc, zc)

    mine = ix if ns > 1 else 0

    def send_side(c):
        return [go(side_ref.at[heights(c)], side_all.at[heights(c), channels(ix), :], "xy", s)
                for s in range(1, ns)]

    side_cp = [send_side(0)]
    front_cp = [go(front_ref, front_all.at[s - 1], "sub", s) for s in range(1, nsub)]
    top_cp = [go(top_ref, top_all.at[s - 1], "gz", s) for s in range(1, ng)]
    side_cp += [send_side(c) for c in range(1, CHUNKS)]

    side_all[:, channels(mine), :] = side_ref[...]
    w = w_ref[...]
    ww[:, 0:L] = w
    ww[:, L:2 * L] = w
    wo = wo_ref[...]
    wp[...] = jnp.zeros_like(wp)
    wp[0:KP, 0:L] = wo
    wp[KP:2 * KP, L:2 * L] = wo
    wl[...] = wp[...].T
    a_side[...] = jnp.zeros_like(a_side)
    a_front[...] = jnp.zeros_like(a_front)
    a_top[...] = jnp.zeros_like(a_top)
    a_gw2[...] = jnp.zeros_like(a_gw2)
    a_gb2[...] = jnp.zeros_like(a_gb2)

    def project_top(plane, owner):
        v = (dot(plane.reshape(xs * yb, L), w) + b_ref[...]) * 0.5
        t_s[:, rows_y(owner), :] = v.reshape(xs, yb, L)

    project_top(top_ref[...], ig)
    for cp in front_cp:
        cp.wait_recv()
    fp = dot(front_ref[...], w_ref[columns(isub), :])
    for s in range(1, nsub):
        fp = fp + dot(front_all[s - 1], w_ref[columns(source("sub", s)), :])
    f_s[...] = (fp * 0.5).reshape(xs, zs, L)
    for s in range(1, ng):
        top_cp[s - 1].wait_recv()
        project_top(top_all[s - 1], source("gz", s))

    iota_k = lax.broadcasted_iota(jnp.int32, (KU, L), 0)
    bo = bo_ref[0:KU, :]
    side_out = []

    for c in range(CHUNKS):
        for cp in side_cp[c]:
            cp.wait_recv()
        for i in range(zc):
            s_s[i] = dot(side_all[c * zc + i], w, 0, 0) * 0.5

        def x_body(xi, _):
            t_x = t_s[xi]
            f_x = f_s[xi, c * zc:(c + 1) * zc, :]
            for z in range(zc):
                p = t_x + (s_s[z] + f_x[z:z + 1])
                t = jnp.tanh(p)
                u = 1.0 + t
                hid = p * u
                at = slice((z // 2) * ys, (z // 2 + 1) * ys), slice((z % 2) * L, (z % 2 + 1) * L)
                g_s[at] = (u + hid * (1.0 - t)).astype(BF16)
                hid_s[at] = hid.astype(BF16)
            logits = dot(hid_s[...], wl[...])
            gb2 = jnp.zeros((KU, L), F32)
            for j in range(pairs):
                lt = logits[j * ys:(j + 1) * ys].T
                for i in range(2):
                    lg = lt[i * KP:i * KP + KU] + bo
                    ex = jnp.exp(lg - jnp.max(lg, axis=0, keepdims=True))
                    prob = ex * (1.0 / jnp.sum(ex, axis=0, keepdims=True))
                    z = c * zc + j * 2 + i
                    dl = prob - jnp.where(iota_k == lab_ref[xi, z:z + 1, :], 1.0, 0.0)
                    gb2 = gb2 + dl
                    dl_s[i * KP:(i + 1) * KP, j * ys:(j + 1) * ys] = jnp.concatenate(
                        [dl, jnp.zeros((KP - KU, L), F32)], axis=0).astype(BF16)
            a_gb2[...] += gb2
            dhid = dot(dl_s[...], wp[...], 0, 0)
            a_gw2[...] += dot(dl_s[...], hid_s[...])
            top_acc = a_top[xi]
            for z in range(zc):
                at = slice((z // 2) * ys, (z // 2 + 1) * ys), slice((z % 2) * L, (z % 2 + 1) * L)
                dpre = dhid[at] * g_s[at].astype(F32)
                a_side[c * zc + z] += dpre
                top_acc = top_acc + dpre
                a_front[xi, c * zc + z:c * zc + z + 1, :] = jnp.sum(dpre, axis=0, keepdims=True)
            a_top[xi] = top_acc
            return 0

        lax.fori_loop(0, xs, x_body, 0)

        for i in range(zc):
            z = c * zc + i
            v = a_side[z] * 0.5
            hi, lo = split(v)
            g = dot(ww[...], jnp.concatenate([hi, lo], axis=1), 1, 1)
            side_snd[z] = g.astype(BF16)
            g_side[i] = g
            a_side[z] = v
        oside_ref[heights(c)] = g_side[:, channels(mine), :]
        for s in range(1, ns):
            side_out.append((c, s, go(side_snd.at[heights(c), channels(peer("xy", s)), :],
                                      side_rcv.at[s - 1, heights(c)], "xy", s)))

    top_out = []
    for s in range(1, ng):
        rows = a_top[:, rows_y(peer("gz", s)), :].reshape(xs * yb, L) * 0.5
        hi, lo = split(rows)
        top_snd[s - 1] = dot(jnp.concatenate([hi, lo], axis=1), ww[...], 1, 1).astype(BF16).reshape(xs, yb, L)
        top_out.append(go(top_snd.at[s - 1], top_rcv.at[s - 1], "gz", s))

    front_sum = a_front[...].reshape(xs * zs, L) * 0.5
    fhi, flo = split(front_sum)
    fcat = jnp.concatenate([fhi, flo], axis=1)
    front_out = []
    for s in range(1, nsub):
        front_snd[s - 1] = dot(fcat, ww[columns(peer("sub", s)), :], 1, 1)
        front_out.append(go(front_snd.at[s - 1], front_rcv.at[s - 1], "sub", s))

    gw1 = jnp.zeros((L, L), F32)
    for z in range(zs):
        gw1 = gw1 + dot(side_all[z], a_side[z].astype(BF16))
    for s in range(ng):
        plane = top_ref[...] if s == 0 else top_all[s - 1]
        own = ig if s == 0 else source("gz", s)
        rows = (a_top[:, rows_y(own), :] * 0.5).reshape(xs * yb, L).astype(BF16)
        gw1 = gw1 + dot(plane.reshape(xs * yb, L), rows, 0, 0)
    gw_loc[0:L, :] = gw1
    for s in range(nsub):
        plane = front_ref[...] if s == 0 else front_all[s - 1]
        at = columns(isub if s == 0 else source("sub", s))
        gw_loc[at, :] = gw_loc[at, :] + dot(plane, fhi, 0, 0)
    gw_loc[L:L + KU, :] = a_gw2[0:KU, 0:L] + a_gw2[KP:KP + KU, L:2 * L]
    gb1 = jnp.sum(front_sum, axis=0, keepdims=True)
    gb2 = jnp.sum(a_gb2[...], axis=1, keepdims=True)
    eye = (lax.broadcasted_iota(jnp.int32, (KU, L), 0) == lax.broadcasted_iota(jnp.int32, (KU, L), 1)).astype(F32)
    gb2_row = jnp.sum(gb2 * eye, axis=0, keepdims=True)
    gw_loc[L + KU:L + KU + 8, :] = jnp.concatenate([gb1, gb2_row, jnp.zeros((6, L), F32)], axis=0)

    hr = (L + KU + 8) // nsub

    def rows_of(i):
        return pl.ds(pl.multiple_of(i * hr, hr), hr)

    cps = [go(gw_loc.at[rows_of(peer("sub", s))], gw_sub.at[s - 1], "sub", s) for s in range(1, nsub)]
    part = gw_loc[rows_of(isub), :]
    for s in range(1, nsub):
        cps[s - 1].wait_recv()
        part = part + gw_sub[s - 1]
    gw_gz[ig] = part
    cps = [go(gw_gz.at[ig], gw_gz.at[ig], "gz", s) for s in range(1, ng)]
    hi, lo = split(a_top[:, rows_y(ig), :].reshape(xs * yb, L) * 0.5)
    otop_ref[...] = dot(jnp.concatenate([hi, lo], axis=1), ww[...], 1, 1).reshape(xs, yb, L)
    ofront_ref[...] = dot(fcat, ww[columns(isub), :], 1, 1)
    for cp in cps:
        cp.wait_recv()
    part = gw_gz[0]
    for j in range(1, ng):
        part = part + gw_gz[j]
    gw_xy[ix] = part * (1.0 / total)
    cps = [go(gw_xy.at[ix], gw_xy.at[ix], "xy", s) for s in range(1, nx)]
    for s in range(1, nsub):
        front_out[s - 1].wait_recv()
        ofront_ref[...] += front_rcv[s - 1]
    for s in range(1, ng):
        top_out[s - 1].wait_recv()
        otop_ref[...] += top_rcv[s - 1].astype(F32)
    for c, s, cp in side_out:
        cp.wait_recv()
        oside_ref[heights(c)] += side_rcv[s - 1, heights(c)].astype(F32)
    for cp in cps:
        cp.wait_recv()
    full = gw_xy[0]
    for j in range(1, nx):
        full = full + gw_xy[j]
    gw_full[rows_of(isub), :] = full
    cps = [go(gw_full.at[rows_of(isub)], gw_full.at[rows_of(isub)], "sub", s) for s in range(1, nsub)]
    for cp in cps:
        cp.wait_recv()
    ogw1_ref[...] = gw_full[0:L, :]
    ogw2_ref[...] = gw_full[L:L + k, :]
    ogb_ref[...] = gw_full[L + KU:L + KU + 8, :]
    for cp in started:
        cp.wait_send()


def on_device(nx, ng, nsub, top, front, side, labels, w_in, b_in, w_out, b_out):
    xs, zs, ys = labels.shape
    total = xs * zs * ys * nx * ng * nsub
    k = w_out.shape[1]
    ns = nx if L // nx >= 16 else 1
    if ns == 1:
        side = lax.all_gather(side, "xy", axis=2, tiled=True)
    cs, cf = L // ns, L // nsub
    wo = jnp.zeros((KP, L), BF16).at[:k].set(w_out.T)
    bo = jnp.full((KP, L), -1e30, F32).at[:k].set(jnp.broadcast_to(b_out[:, None], (k, L)))
    gr = L + KU + 8
    rows = zs // CHUNKS // 2 * ys
    copies = CHUNKS * (ns - 1) * 2 + (ng - 1) * 3 + (nsub - 1) * 4 + (nx - 1)
    cfg = (ns, nx, ng, nsub, xs, zs, ys, k, total)
    vm = pl.BlockSpec(memory_space=pltpu.VMEM)
    V = pltpu.VMEM
    one = max(ns - 1, 1)
    otop, ofront, oside, ogw1, ogw2, ogb = pl.pallas_call(
        functools.partial(kernel, cfg),
        out_shape=(
            jax.ShapeDtypeStruct(top.shape, F32),
            jax.ShapeDtypeStruct((xs * zs, cf), F32),
            jax.ShapeDtypeStruct((zs, cs, ys), F32),
            jax.ShapeDtypeStruct((L, L), F32),
            jax.ShapeDtypeStruct((k, L), F32),
            jax.ShapeDtypeStruct((8, L), F32),
        ),
        in_specs=[vm] * 8,
        out_specs=(vm,) * 6,
        scratch_shapes=[
            V((ng - 1,) + top.shape, BF16), V((nsub - 1, xs * zs, cf), BF16), V((zs, L, ys), BF16),
            V((2 * KP, 2 * L), BF16), V((2 * L, 2 * KP), BF16), V((L, 2 * L), BF16),
            V((xs, ys, L), F32), V((xs, zs, L), F32), V((zs // CHUNKS, ys, L), F32),
            V((rows, 2 * L), BF16), V((rows, 2 * L), BF16), V((2 * KP, rows), BF16),
            V((zs // CHUNKS, L, ys), F32),
            V((xs, ys, L), F32), V((xs, zs, L), F32), V((zs, ys, L), F32),
            V((2 * KP, 2 * L), F32), V((KU, L), F32),
            V((ng - 1,) + top.shape, BF16), V((ng - 1,) + top.shape, BF16),
            V((nsub - 1, xs * zs, cf), F32), V((nsub - 1, xs * zs, cf), F32),
            V((zs, L, ys), BF16), V((one, zs, cs, ys), BF16),
            V((gr, L), F32), V((nsub - 1, gr // nsub, L), F32),
            V((ng, gr // nsub, L), F32), V((nx, gr // nsub, L), F32), V((gr, L), F32),
            pltpu.SemaphoreType.DMA((copies,)), pltpu.SemaphoreType.DMA((copies,)),
        ],
        compiler_params=pltpu.CompilerParams(
            collective_id=0, has_side_effects=True, vmem_limit_bytes=48 * 1024 * 1024),
    )(top, front.reshape(xs * zs, cf), side.transpose(1, 2, 0), labels, w_in, b_in.reshape(1, L), wo, bo)
    gside = oside.transpose(2, 0, 1)
    if ns == 1:
        gside = lax.psum_scatter(gside, "xy", scatter_dimension=2, tiled=True)
    return (otop, ofront.reshape(front.shape), gside, ogw1, ogb[0], ogw2.T, ogb[1, :k])


def solution(mesh):
    in_specs = (
        P(("groups", "xy"), ("sub", "gz"), None),
        P(("groups", "xy"), "gz", "sub"),
        P(("groups", "sub"), "gz", "xy"),
        P(("groups", "xy"), "gz", "sub"),
        P(),
        P(),
        P(),
        P(),
    )
    out_specs = (
        P(("groups", "xy"), ("sub", "gz"), None),
        P(("groups", "xy"), "gz", "sub"),
        P(("groups", "sub"), "gz", "xy"),
        P("groups", None),
        P("groups"),
        P("groups", None),
        P("groups"),
    )
    body = functools.partial(on_device, mesh.shape["xy"], mesh.shape["gz"], mesh.shape["sub"])
    return jax.shard_map(body, mesh=mesh, in_specs=in_specs, out_specs=out_specs, check_vma=False)
```

time: 231 us -> 62.2 us (0.27); the launches traced: 228 us -> 61.9 us
  blocking collectives: 86.4 us -> 0 us
  Pallas kernels: 0 us -> 51.1 us
  matrix products: 41.6 us -> 0 us
  waiting for transfers between devices: 27.6 us -> 0 us
  other arithmetic: 22.5 us -> 0 us
  local copies, waits for them, and re-layouts: 32.4 us -> 10.1 us
  between operations: 15.8 us -> 0.66 us
    psum x1 -> x0, blocking collectives: 58.7 us -> none  [on_device(): gw1, gb1, gw2, gb2 = lax.psum((gw1, gb1, gw2, gb2), ('xy', 'gz', 'sub'))]
    pallas_call x0 -> x1, Pallas kernels: none -> 51.1 us  [on_device(): pl.pallas_call(functools.partial(kernel, cfg), out_shape=(jax.ShapeDtypeS...]
    dot_general x96 -> x0, matrix products: 41.6 us -> none  [the longest x16 10.3 us: step(): lax.dot_general(dpre, w_in, (((1,), (1,)), ((), ())), preferred_element_t...]
    all_gather x3 -> x0, blocking collectives: 27.7 us -> none  [the longest x1 17.5 us: on_device(): side_full = lax.all_gather(side_plane, 'xy', axis=2, tiled=True)]
    psum x1 -> x0, waiting for transfers between devices: 27.1 us -> none  [on_device(): gw1, gb1, gw2, gb2 = lax.psum((gw1, gb1, gw2, gb2), ('xy', 'gz', 'sub'))]
    convert_element_type x32 -> x0, other arithmetic: 14.2 us -> none  [the longest x16 12.3 us: step(): top_row[:, None, :].astype(jnp.float32)]
    dynamic_slice x32 -> x0, local copies, waits for them, and re-layouts: 12.8 us -> none  [on_device(): carry, outs = lax.scan(step, init, (top_full, front_full, labels))]
    dynamic_update_slice x32 -> x0, local copies, waits for them, and re-layouts: 10.2 us -> none  [on_device(): carry, outs = lax.scan(step, init, (top_full, front_full, labels))]
  transfers between devices with their start and end apart: 4 -> 0, of which waited for: 1 -> 0; matrix products, arithmetic and copies ran while one was open for 4% -> 0% of each run, Pallas kernels for 0% -> 0%
where the time goes in v2:
time: 62.2 us; the launch traced here: 61.9 us
  Pallas kernels  51.1 us (82%)
  local copies, waits for them, and re-layouts  10.1 us (16%)
  between operations  0.66 us (1%)
    pallas_call x1, Pallas kernels, on_device(): pl.pallas_call(functools.partial(kernel, cfg), out_shape=(jax.ShapeDtypeS...  51.1 us
    unnamed x17, local copies, waits for them, and re-layouts  7.63 us

profile of v2, /device:TPU:0, one launch (start us, length us, event | category | flops | bytes accessed | tf_op | source)
XLA Modules:
  0.0 61.9 jit_solution(10306176117750795748)
XLA Ops:
  0.6 0.0 copy-start.4
  0.6 0.7 %scatter.13 = f32[32]{0:T(128)S(1)} pad(f32[18]{0:T(128)} %param.19, f32[]{:T(128)} %constant.48.clone.1), padding=0_14 | pad | bytes 204 | tf_op jit(solution)/shard_map/scatter | solution.py:277
  1.3 0.1 scatter.14.bo_ref
  1.4 0.7 %scatter.12.wo_ref = bf16[32,128]{1,0:T(8,128)(2,1)S(1)} pad(bf16[18,128]{1,0:T(8,128)(2,1)} %bitcast.17, bf16[]{:T(256)} %constant.47.clone.1), padding=0_14x0_0 | pad | bytes 12802 | tf_op jit(solution)/shard_map/scatter | solution.py:276
  2.1 0.0 copy-start.5
  2.1 0.0 copy-done.4
  2.1 0.6 %copy-done.5 = f32[128]{0:T(128)S(1)} copy-done((f32[128]{0:T(128)S(1)}, f32[128]{0:T(128)}, u32[]{:S(2)}) %copy-start.5) | copy-done | bytes 536
  2.7 0.0 copy-start
  2.7 0.9 %copy-done = bf16[16,64,128]{2,1,0:T(8,128)(2,1)S(1)} copy-done((bf16[16,64,128]{2,1,0:T(8,128)(2,1)S(1)}, bf16[16,64,128]{2,1,0:T(8,128)(2,1)}, u32[]{:S(2)}) %copy-start) | copy-done | bytes 262168
  3.7 0.0 copy-start.1
  3.7 0.9 %copy-done.1 = bf16[128,16,32]{0,2,1:T(8,128)(2,1)S(1)} copy-done((bf16[128,16,32]{0,2,1:T(8,128)(2,1)S(1)}, bf16[128,16,32]{0,2,1:T(8,128)(2,1)}, u32[]{:S(2)}) %copy-start.1) | copy-done | bytes 131096
  4.6 0.0 copy-start.2
  4.6 0.9 %copy-done.2 = s32[16,16,128]{2,1,0:T(8,128)S(1)} copy-done((s32[16,16,128]{2,1,0:T(8,128)S(1)}, s32[16,16,128]{2,1,0:T(8,128)}, u32[]{:S(2)}) %copy-start.2) | copy-done | bytes 131096
  5.5 0.0 copy-start.3
  5.5 0.8 %copy-done.3 = bf16[16,16,64]{2,1,0:T(8,128)(2,1)S(1)} copy-done((bf16[16,16,64]{2,1,0:T(8,128)(2,1)S(1)}, bf16[16,16,64]{2,1,0:T(8,128)(2,1)}, u32[]{:S(2)}) %copy-start.3) | copy-done | bytes 32792
  6.3 51.1 %shard_map.135 = (f32[16,64,128]{2,1,0:T(8,128)S(1)}, f32[256,64]{1,0:T(8,128)S(1)}, f32[16,32,128]{2,1,0:T(8,128)S(1)}, f32[128,128]{1,0:T(8,128)S(1)}, f32[18,128]{1,0:T(8,128)S(1)}, /*index=5*/f32[8,128]{1,0:T(8,128)S(1)}) custom-call(bf16[16,64,128]{2,1,0:T(8,128)(2,1)S(1)} %copy-done, bf16[256,64]{1,0:T(8,128)(2,1)S(1)} %bitcast.14, ...), custom_call_target="tpu_custom_call" | custom-call | tf_op jit(solution)/shard_map/pallas_call | solution.py:285
  57.5 0.5 slice_bitcast_fusion
  58.0 0.5 slice_bitcast_fusion.1
  58.5 0.8 %copy.20 = f32[16,64,128]{2,1,0:T(8,128)} copy(f32[16,64,128]{2,1,0:T(8,128)S(1)} %get-tuple-element.50) | data formatting | bytes 1048576
  59.3 0.7 %copy.21 = f32[16,16,64]{2,1,0:T(8,128)} copy(f32[16,16,64]{2,1,0:T(8,128)S(1)} %bitcast.12) | data formatting | bytes 131072
  59.9 0.7 %copy.22 = f32[128,16,32]{0,2,1:T(8,128)} copy(f32[128,16,32]{0,2,1:T(8,128)S(1)} %bitcast.11) | data formatting | bytes 524288
  60.6 0.6 %copy.23 = f32[128,128]{1,0:T(8,128)} copy(f32[128,128]{1,0:T(8,128)S(1)} %get-tuple-element.53) | data formatting | bytes 131072
  61.3 0.6 copy.24
Async XLA Ops:
  0.6 1.5 %copy-start.4 = (bf16[128,128]{1,0:T(8,128)(2,1)S(1)}, bf16[128,128]{1,0:T(8,128)(2,1)}, u32[]{:S(2)}) copy-start(bf16[128,128]{1,0:T(8,128)(2,1)} %w_ref.1) | copy-start | bytes 98308
  2.1 0.7 %copy-start.5 = (f32[128]{0:T(128)S(1)}, f32[128]{0:T(128)}, u32[]{:S(2)}) copy-start(f32[128]{0:T(128)} %param.17) | copy-start | bytes 1540
  2.7 0.9 %copy-start = (bf16[16,64,128]{2,1,0:T(8,128)(2,1)S(1)}, bf16[16,64,128]{2,1,0:T(8,128)(2,1)}, u32[]{:S(2)}) copy-start(bf16[16,64,128]{2,1,0:T(8,128)(2,1)} %top_ref.1) | copy-start | bytes 786436
  3.7 0.9 %copy-start.1 = (bf16[128,16,32]{0,2,1:T(8,128)(2,1)S(1)}, bf16[128,16,32]{0,2,1:T(8,128)(2,1)}, u32[]{:S(2)}) copy-start(bf16[128,16,32]{0,2,1:T(8,128)(2,1)} %param.14) | copy-start | bytes 393220
  4.6 0.9 %copy-start.2 = (s32[16,16,128]{2,1,0:T(8,128)S(1)}, s32[16,16,128]{2,1,0:T(8,128)}, u32[]{:S(2)}) copy-start(s32[16,16,128]{2,1,0:T(8,128)} %lab_ref.1) | copy-start | bytes 393220
  5.5 0.8 %copy-start.3 = (bf16[16,16,64]{2,1,0:T(8,128)(2,1)S(1)}, bf16[16,16,64]{2,1,0:T(8,128)(2,1)}, u32[]{:S(2)}) copy-start(bf16[16,16,64]{2,1,0:T(8,128)(2,1)} %param.13) | copy-start | bytes 98308

commit v3 on v2

v3 whole, which is shorter than its diff:
```python
import functools

import jax
import jax.numpy as jnp
from jax import lax
from jax.experimental import pallas as pl
from jax.experimental.pallas import tpu as pltpu
from jax.sharding import PartitionSpec as P

F32 = jnp.float32
BF16 = jnp.bfloat16
KP = 32
KU = 24
L = 128
CHUNKS = 4
SEGMENTS = 4
UNROLL = 2


def dot(a, b, ca=1, cb=0):
    return lax.dot_general(a, b, (((ca,), (cb,)), ((), ())), preferred_element_type=F32)


def split(v):
    hi = v.astype(BF16)
    return hi, (v - hi.astype(F32)).astype(BF16)


def kernel(cfg, top_hbm, front_ref, side_ref, lab_hbm, w_ref, b_ref, wo_ref, bo_ref,
           otop_ref, ofront_ref, oside_ref, ogw1_ref, ogw2_ref, ogb1_ref, ogb2_ref,
           top_ref, lab_ref, top_all, front_all, side_all, wp, wl, ww, t_s, f_s, s_s, hid_s, g_s, dl_s, g_side,
           a_top, a_front, a_side, a_gw2, a_gb2,
           top_snd, top_rcv, front_snd, front_rcv, side_snd, side_rcv,
           gw_loc, gw_sub, gw_gz, gw_xy, gw_full,
           sem_s, sem_r, sem_l):
    ns, nx, ng, nsub, xs, zs, ys, k, total = cfg
    ix, ig, isub = lax.axis_index("xy"), lax.axis_index("gz"), lax.axis_index("sub")
    ids = {"xy": (ix, nx), "gz": (ig, ng), "sub": (isub, nsub)}
    cs, cf = L // ns, L // nsub
    zc = zs // CHUNKS
    pairs = zc // 2
    yb = top_ref.shape[1]
    xc = xs // SEGMENTS

    def peer(axis, s):
        me, n = ids[axis]
        return lax.rem(me + s, n)

    def source(axis, s):
        me, n = ids[axis]
        return lax.rem(me + n - s, n)

    counter = [0]
    started = []

    def go(src, dst, axis, s):
        i = counter[0]
        counter[0] += 1
        copy = pltpu.make_async_remote_copy(
            src_ref=src, dst_ref=dst, send_sem=sem_s.at[i], recv_sem=sem_r.at[i],
            device_id={axis: peer(axis, s)}, device_id_type=pl.DeviceIdType.MESH)
        copy.start()
        started.append(copy)
        return copy

    def local(src, dst, i):
        copy = pltpu.make_async_copy(src, dst, sem_l.at[i])
        copy.start()
        return copy

    def channels(i):
        return pl.ds(pl.multiple_of(i * cs, cs), cs)

    def columns(i):
        return pl.ds(pl.multiple_of(i * cf, cf), cf)

    def rows_y(i):
        return pl.ds(pl.multiple_of(i * yb, yb), yb)

    def heights(c):
        return pl.ds(c * zc, zc)

    mine = ix if ns > 1 else 0

    def run(g):
        return pl.ds(g * xc, xc)

    def send_side(c):
        return [go(side_ref.at[heights(c)], side_all.at[heights(c), channels(ix), :], "xy", s)
                for s in range(1, ns)]

    loc_top = local(top_hbm, top_ref, 0)
    loc_side = local(side_ref, side_all.at[:, channels(mine), :], 1)
    loc_lab = local(lab_hbm, lab_ref, 2)

    bar = pltpu.get_barrier_semaphore()
    greet = 0
    for axis in ("sub", "gz", "xy"):
        for s in range(1, ids[axis][1]):
            pl.semaphore_signal(bar, inc=1, device_id={axis: peer(axis, s)}, device_id_type=pl.DeviceIdType.MESH)
            greet += 1
    pl.semaphore_wait(bar, greet)

    side_cp = [send_side(0)]
    front_cp = [go(front_ref, front_all.at[s - 1], "sub", s) for s in range(1, nsub)]
    top_cp = [[go(top_hbm.at[run(g)], top_all.at[s - 1, run(g)], "gz", s) for s in range(1, ng)]
              for g in range(SEGMENTS)]
    side_cp += [send_side(c) for c in range(1, CHUNKS)]

    w = w_ref[...]
    ww[:, 0:L] = w
    ww[:, L:2 * L] = w
    wp[...] = jnp.zeros_like(wp)
    wp[0:k, 0:L] = wo_ref[...]
    wp[KP:KP + k, L:2 * L] = wo_ref[...]
    wl[...] = wp[...].T
    gw_loc[...] = jnp.zeros_like(gw_loc)
    a_side[...] = jnp.zeros_like(a_side)
    a_front[...] = jnp.zeros_like(a_front)
    a_top[...] = jnp.zeros_like(a_top)
    a_gw2[...] = jnp.zeros_like(a_gw2)
    a_gb2[...] = jnp.zeros_like(a_gb2)

    def project_top(plane, owner, g):
        v = (dot(plane.reshape(xc * yb, L), w) + b_ref[...]) * 0.5
        t_s[run(g), rows_y(owner), :] = v.reshape(xc, yb, L)

    loc_top.wait()
    for g in range(SEGMENTS):
        project_top(top_ref[run(g)], ig, g)
    for cp in front_cp:
        cp.wait_recv()
    fp = dot(front_ref[...], w_ref[columns(isub), :])
    for s in range(1, nsub):
        fp = fp + dot(front_all[s - 1], w_ref[columns(source("sub", s)), :])
    f_s[...] = (fp * 0.5).reshape(xs, zs, L)
    iota_k = lax.broadcasted_iota(jnp.int32, (KU, L), 0)
    eye = (iota_k == lax.broadcasted_iota(jnp.int32, (KU, L), 1)).astype(F32)
    bias = jnp.sum(eye * bo_ref[...], axis=1, keepdims=True)
    bo = jnp.where(iota_k < k, jnp.broadcast_to(bias, (KU, L)), -1e30)
    loc_side.wait()
    loc_lab.wait()
    top_out = []
    side_out = []

    hr = (L + KU + 8) // nsub

    def rows_of(i):
        return pl.ds(pl.multiple_of(i * hr, hr), hr)

    def finish_top(g):
        gw1 = jnp.zeros((L, L), F32)
        for s in list(range(1, ng)) + [0]:
            own = peer("gz", s)
            rows = a_top[run(g), rows_y(own), :].reshape(xc * yb, L) * 0.5
            hi, lo = split(rows)
            v = dot(jnp.concatenate([hi, lo], axis=1), ww[...], 1, 1).reshape(xc, yb, L)
            if s > 0:
                top_snd[s - 1, run(g)] = v.astype(BF16)
                top_out.append((g, s, go(top_snd.at[s - 1, run(g)], top_rcv.at[s - 1, run(g)], "gz", s)))
                plane = top_all[ng - s - 1, run(g)]
            else:
                otop_ref[run(g)] = v
                plane = top_ref[run(g)]
            gw1 = gw1 + dot(plane.reshape(xc * yb, L), hi, 0, 0)
        gw_loc[0:L, :] += gw1

    gw_sub_cp = []

    def start_weights():
        front_sum = a_front[...].reshape(xs * zs, L) * 0.5
        fhi = front_sum.astype(BF16)
        gw1 = jnp.zeros((L, L), F32)
        for z in range(zs):
            gw1 = gw1 + dot(side_all[z], (a_side[z] * 0.5).astype(BF16))
        gw_loc[0:L, :] += gw1
        for s in range(nsub):
            plane = front_ref[...] if s == 0 else front_all[s - 1]
            at = columns(isub if s == 0 else source("sub", s))
            gw_loc[at, :] = gw_loc[at, :] + dot(plane, fhi, 0, 0)
        gw_loc[L:L + KU, :] = a_gw2[0:KU, 0:L] + a_gw2[KP:KP + KU, L:2 * L]
        gb1 = jnp.sum(front_sum, axis=0, keepdims=True)
        gb2 = jnp.sum(a_gb2[...], axis=1, keepdims=True)
        gb2_row = jnp.sum(gb2 * eye, axis=0, keepdims=True)
        gw_loc[L + KU:L + KU + 8, :] = jnp.concatenate([gb1, gb2_row, jnp.zeros((6, L), F32)], axis=0)
        gw_sub_cp.extend(go(gw_loc.at[rows_of(peer("sub", s))], gw_sub.at[s - 1], "sub", s) for s in range(1, nsub))
        part = gw_loc[rows_of(isub), :]
        for s in range(1, nsub):
            gw_sub_cp[s - 1].wait_recv()
            part = part + gw_sub[s - 1]
        gw_gz[ig] = part
        gw_gz_cp.extend(go(gw_gz.at[ig], gw_gz.at[ig], "gz", s) for s in range(1, ng))

    gw_gz_cp = []

    for c in range(CHUNKS):
        for cp in side_cp[c]:
            cp.wait_recv()
        for i in range(zc):
            s_s[i] = dot(side_all[c * zc + i], w, 0, 0) * 0.5

        def x_body(xi, _):
            t_x = t_s[xi]
            f_x = f_s[xi, c * zc:(c + 1) * zc, :]
            for z in range(zc):
                p = t_x + (s_s[z] + f_x[z:z + 1])
                t = jnp.tanh(p)
                u = 1.0 + t
                hid = p * u
                at = slice((z // 2) * ys, (z // 2 + 1) * ys), slice((z % 2) * L, (z % 2 + 1) * L)
                g_s[at] = (u + hid * (1.0 - t)).astype(BF16)
                hid_s[at] = hid.astype(BF16)
            logits = dot(hid_s[...], wl[...])
            gb2 = jnp.zeros((KU, L), F32)
            for j in range(pairs):
                lt = logits[j * ys:(j + 1) * ys].T
                for i in range(2):
                    lg = lt[i * KP:i * KP + KU] + bo
                    ex = jnp.exp(lg - jnp.max(lg, axis=0, keepdims=True))
                    prob = ex * (1.0 / jnp.sum(ex, axis=0, keepdims=True))
                    z = c * zc + j * 2 + i
                    dl = prob - jnp.where(iota_k == lab_ref[xi, z:z + 1, :], 1.0, 0.0)
                    gb2 = gb2 + dl
                    dl_s[i * KP:(i + 1) * KP, j * ys:(j + 1) * ys] = jnp.concatenate(
                        [dl, jnp.zeros((KP - KU, L), F32)], axis=0).astype(BF16)
            a_gb2[...] += gb2
            dhid = dot(dl_s[...], wp[...], 0, 0)
            a_gw2[...] += dot(dl_s[...], hid_s[...])
            top_acc = a_top[xi]
            for z in range(zc):
                at = slice((z // 2) * ys, (z // 2 + 1) * ys), slice((z % 2) * L, (z % 2 + 1) * L)
                dpre = dhid[at] * g_s[at].astype(F32)
                a_side[c * zc + z] += dpre
                top_acc = top_acc + dpre
                a_front[xi, c * zc + z:c * zc + z + 1, :] = jnp.sum(dpre, axis=0, keepdims=True)
            a_top[xi] = top_acc
            return 0

        if c == 0 or c == CHUNKS - 1:
            for g in range(SEGMENTS):
                if c == 0:
                    for s in range(1, ng):
                        top_cp[g][s - 1].wait_recv()
                        project_top(top_all[s - 1, run(g)], source("gz", s), g)
                lax.fori_loop(g * xc, (g + 1) * xc, x_body, 0, unroll=UNROLL)
                if c == CHUNKS - 1:
                    finish_top(g)
        else:
            lax.fori_loop(0, xs, x_body, 0, unroll=UNROLL)
        if c == CHUNKS - 1:
            start_weights()

        for i in range(zc):
            z = c * zc + i
            hi, lo = split(a_side[z] * 0.5)
            g = dot(ww[...], jnp.concatenate([hi, lo], axis=1), 1, 1)
            side_snd[z] = g.astype(BF16)
            g_side[i] = g
        oside_ref[heights(c)] = g_side[:, channels(mine), :]
        for s in range(1, ns):
            side_out.append((c, s, go(side_snd.at[heights(c), channels(peer("xy", s)), :],
                                      side_rcv.at[s - 1, heights(c)], "xy", s)))

    fcat = jnp.concatenate(split(a_front[...].reshape(xs * zs, L) * 0.5), axis=1)
    front_out = []
    for s in range(1, nsub):
        front_snd[s - 1] = dot(fcat, ww[columns(peer("sub", s)), :], 1, 1)
        front_out.append(go(front_snd.at[s - 1], front_rcv.at[s - 1], "sub", s))
    ofront_ref[...] = dot(fcat, ww[columns(isub), :], 1, 1)
    for cp in gw_gz_cp:
        cp.wait_recv()
    part = gw_gz[0]
    for j in range(1, ng):
        part = part + gw_gz[j]
    gw_xy[ix] = part * (1.0 / total)
    cps = [go(gw_xy.at[ix], gw_xy.at[ix], "xy", s) for s in range(1, nx)]
    for s in range(1, nsub):
        front_out[s - 1].wait_recv()
        ofront_ref[...] += front_rcv[s - 1]
    for g, s, cp in top_out:
        cp.wait_recv()
        otop_ref[run(g)] += top_rcv[s - 1, run(g)].astype(F32)
    for c, s, cp in side_out:
        cp.wait_recv()
        oside_ref[heights(c)] += side_rcv[s - 1, heights(c)].astype(F32)
    for cp in cps:
        cp.wait_recv()
    full = gw_xy[0]
    for j in range(1, nx):
        full = full + gw_xy[j]
    gw_full[rows_of(isub), :] = full
    cps = [go(gw_full.at[rows_of(isub)], gw_full.at[rows_of(isub)], "sub", s) for s in range(1, nsub)]
    for cp in cps:
        cp.wait_recv()
    ogw1_ref[...] = gw_full[0:L, :]
    ogw2_ref[...] = gw_full[L:L + k, :]
    ogb1_ref[...] = gw_full[L + KU:L + KU + 1, :]
    ogb2_ref[...] = gw_full[L + KU + 1:L + KU + 2, 0:k]
    for cp in started:
        cp.wait_send()


def store(*refs):
    sems = refs[-1]
    n = (len(refs) - 1) // 2
    copies = [pltpu.make_async_copy(refs[i], refs[n + i], sems.at[i]) for i in range(n)]
    for copy in copies:
        copy.start()
    for copy in copies:
        copy.wait()


def on_device(nx, ng, nsub, top, front, side, labels, w_in, b_in, w_out, b_out):
    xs, zs, ys = labels.shape
    total = xs * zs * ys * nx * ng * nsub
    k = w_out.shape[1]
    ns = nx if L // nx >= 16 else 1
    if ns == 1:
        side = lax.all_gather(side, "xy", axis=2, tiled=True)
    cs, cf = L // ns, L // nsub
    bo = jnp.pad(b_out, (0, L - k)).reshape(1, L)
    gr = L + KU + 8
    rows = zs // CHUNKS // 2 * ys
    copies = CHUNKS * (ns - 1) * 2 + (ng - 1) * (2 * SEGMENTS + 1) + (nsub - 1) * 4 + (nx - 1)
    cfg = (ns, nx, ng, nsub, xs, zs, ys, k, total)
    vm = pl.BlockSpec(memory_space=pltpu.VMEM)
    hbm = pl.BlockSpec(memory_space=pl.ANY)
    V = pltpu.VMEM
    one = max(ns - 1, 1)
    outs = pl.pallas_call(
        functools.partial(kernel, cfg),
        out_shape=(
            jax.ShapeDtypeStruct(top.shape, F32),
            jax.ShapeDtypeStruct((xs * zs, cf), F32),
            jax.ShapeDtypeStruct((zs, cs, ys), F32),
            jax.ShapeDtypeStruct((L, L), F32),
            jax.ShapeDtypeStruct((k, L), F32),
            jax.ShapeDtypeStruct((1, L), F32),
            jax.ShapeDtypeStruct((1, k), F32),
        ),
        in_specs=[hbm, vm, hbm, hbm, vm, vm, vm, vm],
        out_specs=(vm,) * 7,
        scratch_shapes=[
            V(top.shape, BF16), V(labels.shape, jnp.int32),
            V((ng - 1,) + top.shape, BF16), V((nsub - 1, xs * zs, cf), BF16), V((zs, L, ys), BF16),
            V((2 * KP, 2 * L), BF16), V((2 * L, 2 * KP), BF16), V((L, 2 * L), BF16),
            V((xs, ys, L), F32), V((xs, zs, L), F32), V((zs // CHUNKS, ys, L), F32),
            V((rows, 2 * L), BF16), V((rows, 2 * L), BF16), V((2 * KP, rows), BF16),
            V((zs // CHUNKS, L, ys), F32),
            V((xs, ys, L), F32), V((xs, zs, L), F32), V((zs, ys, L), F32),
            V((2 * KP, 2 * L), F32), V((KU, L), F32),
            V((ng - 1,) + top.shape, BF16), V((ng - 1,) + top.shape, BF16),
            V((nsub - 1, xs * zs, cf), F32), V((nsub - 1, xs * zs, cf), F32),
            V((zs, L, ys), BF16), V((one, zs, cs, ys), BF16),
            V((gr, L), F32), V((nsub - 1, gr // nsub, L), F32),
            V((ng, gr // nsub, L), F32), V((nx, gr // nsub, L), F32), V((gr, L), F32),
            pltpu.SemaphoreType.DMA((copies,)), pltpu.SemaphoreType.DMA((copies,)),
            pltpu.SemaphoreType.DMA((3,)),
        ],
        compiler_params=pltpu.CompilerParams(
            collective_id=0, has_side_effects=True, vmem_limit_bytes=48 * 1024 * 1024),
    )(top, front.reshape(xs * zs, cf), side.transpose(1, 2, 0), labels, w_in, b_in.reshape(1, L), w_out.T, bo)
    otop, ofront, oside, ogw1, ogw2, ogb1, ogb2 = pl.pallas_call(
        store,
        out_shape=tuple(jax.ShapeDtypeStruct(o.shape, F32) for o in outs),
        in_specs=[vm] * 7,
        out_specs=(hbm,) * 7,
        scratch_shapes=[pltpu.SemaphoreType.DMA((7,))],
    )(*outs)
    gside = oside.transpose(2, 0, 1)
    if ns == 1:
        gside = lax.psum_scatter(gside, "xy", scatter_dimension=2, tiled=True)
    return (otop, ofront.reshape(front.shape), gside, ogw1, ogb1[0], ogw2.T, ogb2[0])


def solution(mesh):
    in_specs = (
        P(("groups", "xy"), ("sub", "gz"), None),
        P(("groups", "xy"), "gz", "sub"),
        P(("groups", "sub"), "gz", "xy"),
        P(("groups", "xy"), "gz", "sub"),
        P(),
        P(),
        P(),
        P(),
    )
    out_specs = (
        P(("groups", "xy"), ("sub", "gz"), None),
        P(("groups", "xy"), "gz", "sub"),
        P(("groups", "sub"), "gz", "xy"),
        P("groups", None),
        P("groups"),
        P("groups", None),
        P("groups"),
    )
    body = functools.partial(on_device, mesh.shape["xy"], mesh.shape["gz"], mesh.shape["sub"])
    return jax.shard_map(body, mesh=mesh, in_specs=in_specs, out_specs=out_specs, check_vma=False)
```

time: 62.2 us -> 64.2 us (1.032)
  Pallas kernels: 51.1 us -> 53.5 us
    pallas_call x0 -> x1, Pallas kernels: none -> 2.21 us  [on_device(): pl.pallas_call(store, out_shape=tuple((jax.ShapeDtypeStruct(o.shape, F32)...]
    unnamed x17 -> x30, local copies, waits for them, and re-layouts: 7.63 us -> 9.62 us
    scatter x3 -> x0, local copies, waits for them, and re-layouts: 1.44 us -> none  [the longest x2 0.74 us: on_device(): jnp.full((KP, L), -1e+30, F32).at[:k]]
    squeeze x2 -> x0, local copies, waits for them, and re-layouts: 1.02 us -> none  [the longest x1 0.51 us: on_device(): ogb[1, :k]]
where the time goes in v3:
time: 64.2 us; the launch traced here: 63.8 us
  Pallas kernels  53.5 us (83%)
  local copies, waits for them, and re-layouts  9.62 us (15%)
  between operations  0.68 us (1%)
    pallas_call x1, Pallas kernels, on_device(): pl.pallas_call(functools.partial(kernel, cfg), out_shape=(jax.ShapeDtypeS...  51.3 us
    unnamed x30, local copies, waits for them, and re-layouts  9.62 us
    pallas_call x1, Pallas kernels, on_device(): pl.pallas_call(store, out_shape=tuple((jax.ShapeDtypeStruct(o.shape, F32)...  2.21 us

profile of v3, /device:TPU:0, one launch (start us, length us, event | category | flops | bytes accessed | tf_op | source)
XLA Modules:
  0.0 63.8 jit_solution(9271484464846504398)
XLA Ops:
  0.6 0.0 copy-start.10
  0.6 0.0 copy-start.14
  0.7 0.7 %copy-done.14 = f32[18]{0:T(128)S(1)} copy-done((f32[18]{0:T(128)S(1)}, f32[18]{0:T(128)}, u32[]{:S(2)}) %copy-start.14) | copy-done | bytes 96
  1.3 0.0 copy-start.11
  1.3 0.0 copy-done.10
  1.3 0.6 copy-done.11
  2.0 0.0 copy-start.1
  2.0 0.9 %copy-done.1 = bf16[16,64,128]{2,1,0:T(8,128)(2,1)S(1)} copy-done((bf16[16,64,128]{2,1,0:T(8,128)(2,1)S(1)}, bf16[16,64,128]{2,1,0:T(8,128)(2,1)}, u32[]{:S(2)}) %copy-start.1) | copy-done | bytes 262168
  2.9 0.0 copy-start.3
  2.9 0.9 %copy-done.3 = bf16[128,16,32]{0,2,1:T(8,128)(2,1)S(1)} copy-done((bf16[128,16,32]{0,2,1:T(8,128)(2,1)S(1)}, bf16[128,16,32]{0,2,1:T(8,128)(2,1)}, u32[]{:S(2)}) %copy-start.3) | copy-done | bytes 131096
  3.8 0.0 copy-start.4
  3.8 0.9 %copy-done.4 = s32[16,16,128]{2,1,0:T(8,128)S(1)} copy-done((s32[16,16,128]{2,1,0:T(8,128)S(1)}, s32[16,16,128]{2,1,0:T(8,128)}, u32[]{:S(2)}) %copy-start.4) | copy-done | bytes 131096
  4.7 0.8 %copy-done.6 = bf16[16,16,64]{2,1,0:T(8,128)(2,1)S(1)} copy-done((bf16[16,16,64]{2,1,0:T(8,128)(2,1)S(1)}, bf16[16,16,64]{2,1,0:T(8,128)(2,1)}, u32[]{:S(2)}) %copy-start.6) | copy-done | bytes 32792
  5.6 0.8 %copy-done.8 = bf16[128,128]{1,0:T(8,128)(2,1)S(1)} copy-done((bf16[128,128]{1,0:T(8,128)(2,1)S(1)}, bf16[128,128]{1,0:T(8,128)(2,1)}, u32[]{:S(2)}) %copy-start.8) | copy-done | bytes 32792
  6.3 51.3 %shard_map.135 = (f32[16,64,128]{2,1,0:T(8,128)S(1)}, f32[256,64]{1,0:T(8,128)S(1)}, f32[16,32,128]{2,1,0:T(8,128)S(1)}, f32[128,128]{1,0:T(8,128)S(1)}, f32[18,...) custom-call(bf16[16,64,128]{2,1,0:T(8,128)(2,1)S(1)} %copy-done.1, bf16[256,64]{1,0:T(8,128)(2,1)S(1)} %bitcast.12, ...), custom_call_target="tpu_custom_call" | custom-call | tf_op jit(solution)/shard_map/pallas_call | solution.py:330
  57.6 0.0 copy-start
  57.6 0.8 %copy-done = f32[16,64,128]{2,1,0:T(8,128)} copy-done((f32[16,64,128]{2,1,0:T(8,128)}, f32[16,64,128]{2,1,0:T(8,128)S(1)}, u32[]{:S(2)}) %copy-start) | copy-done | bytes 524312
  58.4 0.7 %copy-done.2 = f32[16,32,128]{2,1,0:T(8,128)} copy-done((f32[16,32,128]{2,1,0:T(8,128)}, f32[16,32,128]{2,1,0:T(8,128)S(1)}, u32[]{:S(2)}) %copy-start.2) | copy-done | bytes 262168
  59.1 0.6 %copy-done.5 = f32[256,64]{1,0:T(8,128)} copy-done((f32[256,64]{1,0:T(8,128)}, f32[256,64]{1,0:T(8,128)S(1)}, u32[]{:S(2)}) %copy-start.5) | copy-done | bytes 65560
  59.8 0.6 copy-done.7
  60.4 0.6 copy-done.9
  61.0 0.5 copy-done.12
  61.5 0.1 copy-done.13
  61.6 2.2 %shard_map.136 = (f32[16,64,128]{2,1,0:T(8,128)}, f32[256,64]{1,0:T(8,128)}, f32[16,32,128]{2,1,0:T(8,128)}, f32[128,128]{1,0:T(8,128)}, f32[18,128]{1,0:T(8,128)}, /*index=5*/f32[1,128]{1,0:T(1,128)}, f32[1,18]{1,0:T(1,128)}) custom-call(f32[16,64,128]{2,1,0:T(8,128)} %copy-done, f32[256,64]{1,0:T(8,128)} %copy-done.5, f32[16,32,128]{2,1,0:T(8,128)} %copy-done.2, ...), custom_call_target="tpu_custom_call" | custom-call | tf_op jit(solution)/shard_map/pallas_call | solution.py:363
  (9 shorter events, 0.0 us)
Async XLA Ops:
  0.6 0.7 %copy-start.10 = (bf16[128,18]{0,1:T(8,128)(2,1)S(1)}, bf16[128,18]{0,1:T(8,128)(2,1)}, u32[]{:S(2)}) copy-start(bf16[128,18]{0,1:T(8,128)(2,1)} %param.14) | copy-start | bytes 13828
  0.6 0.7 %copy-start.14 = (f32[18]{0:T(128)S(1)}, f32[18]{0:T(128)}, u32[]{:S(2)}) copy-start(f32[18]{0:T(128)} %param.15) | copy-start | bytes 220
  1.3 0.7 %copy-start.11 = (f32[128]{0:T(128)S(1)}, f32[128]{0:T(128)}, u32[]{:S(2)}) copy-start(f32[128]{0:T(128)} %param.13) | copy-start | bytes 1540
  2.0 0.9 %copy-start.1 = (bf16[16,64,128]{2,1,0:T(8,128)(2,1)S(1)}, bf16[16,64,128]{2,1,0:T(8,128)(2,1)}, u32[]{:S(2)}) copy-start(bf16[16,64,128]{2,1,0:T(8,128)(2,1)} %top_hbm.1) | copy-start | bytes 786436
  2.9 0.9 %copy-start.3 = (bf16[128,16,32]{0,2,1:T(8,128)(2,1)S(1)}, bf16[128,16,32]{0,2,1:T(8,128)(2,1)}, u32[]{:S(2)}) copy-start(bf16[128,16,32]{0,2,1:T(8,128)(2,1)} %param.10) | copy-start | bytes 393220
  3.8 0.9 %copy-start.4 = (s32[16,16,128]{2,1,0:T(8,128)S(1)}, s32[16,16,128]{2,1,0:T(8,128)}, u32[]{:S(2)}) copy-start(s32[16,16,128]{2,1,0:T(8,128)} %lab_hbm.1) | copy-start | bytes 393220
  4.7 0.8 %copy-start.6 = (bf16[16,16,64]{2,1,0:T(8,128)(2,1)S(1)}, bf16[16,16,64]{2,1,0:T(8,128)(2,1)}, u32[]{:S(2)}) copy-start(bf16[16,16,64]{2,1,0:T(8,128)(2,1)} %param.9) | copy-start | bytes 98308
  5.6 0.8 %copy-start.8 = (bf16[128,128]{1,0:T(8,128)(2,1)S(1)}, bf16[128,128]{1,0:T(8,128)(2,1)}, u32[]{:S(2)}) copy-start(bf16[128,128]{1,0:T(8,128)(2,1)} %w_ref.1) | copy-start | bytes 98308
  57.6 0.8 %copy-start = (f32[16,64,128]{2,1,0:T(8,128)}, f32[16,64,128]{2,1,0:T(8,128)S(1)}, u32[]{:S(2)}) copy-start(f32[16,64,128]{2,1,0:T(8,128)S(1)} %get-tuple-element.21.refs_0_) | copy-start | bytes 1572868
  58.4 0.7 %copy-start.2 = (f32[16,32,128]{2,1,0:T(8,128)}, f32[16,32,128]{2,1,0:T(8,128)S(1)}, u32[]{:S(2)}) copy-start(f32[16,32,128]{2,1,0:T(8,128)S(1)} %get-tuple-element.23.refs_2_) | copy-start | bytes 786436
  59.1 0.7 %copy-start.5 = (f32[256,64]{1,0:T(8,128)}, f32[256,64]{1,0:T(8,128)S(1)}, u32[]{:S(2)}) copy-start(f32[256,64]{1,0:T(8,128)S(1)} %get-tuple-element.22.refs_1_) | copy-start | bytes 196612
  59.8 0.6 copy-start.7
  60.4 0.6 copy-start.9
  61.0 0.5 copy-start.12
  61.0 0.6 copy-start.13

commit v4 on v2

--- a/solution.py
+++ b/solution.py
@@ -95,10 +95,9 @@
     w = w_ref[...]
     ww[:, 0:L] = w
     ww[:, L:2 * L] = w
-    wo = wo_ref[...]
     wp[...] = jnp.zeros_like(wp)
-    wp[0:KP, 0:L] = wo
-    wp[KP:2 * KP, L:2 * L] = wo
+    wp[0:k, 0:L] = wo_ref[...]
+    wp[KP:KP + k, L:2 * L] = wo_ref[...]
     wl[...] = wp[...].T
     a_side[...] = jnp.zeros_like(a_side)
     a_front[...] = jnp.zeros_like(a_front)
@@ -122,7 +121,9 @@
         project_top(top_all[s - 1], source("gz", s))
 
     iota_k = lax.broadcasted_iota(jnp.int32, (KU, L), 0)
-    bo = bo_ref[0:KU, :]
+    eye = (iota_k == lax.broadcasted_iota(jnp.int32, (KU, L), 1)).astype(F32)
+    bias = jnp.sum(eye * bo_ref[...], axis=1, keepdims=True)
+    bo = jnp.where(iota_k < k, jnp.broadcast_to(bias, (KU, L)), -1e30)
     side_out = []
 
     for c in range(CHUNKS):
@@ -168,7 +169,7 @@
             a_top[xi] = top_acc
             return 0
 
-        lax.fori_loop(0, xs, x_body, 0)
+        lax.fori_loop(0, xs, x_body, 0, unroll=2)
 
         for i in range(zc):
             z = c * zc + i
@@ -273,8 +274,7 @@
     if ns == 1:
         side = lax.all_gather(side, "xy", axis=2, tiled=True)
     cs, cf = L // ns, L // nsub
-    wo = jnp.zeros((KP, L), BF16).at[:k].set(w_out.T)
-    bo = jnp.full((KP, L), -1e30, F32).at[:k].set(jnp.broadcast_to(b_out[:, None], (k, L)))
+    bo = jnp.pad(b_out, (0, L - k)).reshape(1, L)
     gr = L + KU + 8
     rows = zs // CHUNKS // 2 * ys
     copies = CHUNKS * (ns - 1) * 2 + (ng - 1) * 3 + (nsub - 1) * 4 + (nx - 1)
@@ -310,8 +310,8 @@
             pltpu.SemaphoreType.DMA((copies,)), pltpu.SemaphoreType.DMA((copies,)),
         ],
         compiler_params=pltpu.CompilerParams(
-            collective_id=0, has_side_effects=True, vmem_limit_bytes=48 * 1024 * 1024),
-    )(top, front.reshape(xs * zs, cf), side.transpose(1, 2, 0), labels, w_in, b_in.reshape(1, L), wo, bo)
+            collective_id=0, has_side_effects=True, vmem_limit_bytes=60 * 1024 * 1024),
+    )(top, front.reshape(xs * zs, cf), side.transpose(1, 2, 0), labels, w_in, b_in.reshape(1, L), w_out.T, bo)
     gside = oside.transpose(2, 0, 1)
     if ns == 1:
         gside = lax.psum_scatter(gside, "xy", scatter_dimension=2, tiled=True)

time: 62.2 us -> 62.3 us (level)
  Pallas kernels: 51.1 us -> 52.7 us
  local copies, waits for them, and re-layouts: 10.1 us -> 8.62 us
    unnamed x17 -> x13, local copies, waits for them, and re-layouts: 7.63 us -> 5.09 us
    pallas_call x1, Pallas kernels: 51.1 us -> 52.7 us  [on_device(): pl.pallas_call(functools.partial(kernel, cfg), out_shape=(jax.ShapeDtypeS...]
    scatter x3 -> x0, local copies, waits for them, and re-layouts: 1.44 us -> none  [the longest x2 0.74 us: on_device(): jnp.full((KP, L), -1e+30, F32).at[:k]]
    reshape x0 -> x1, local copies, waits for them, and re-layouts: none -> 1.17 us  [on_device(): bo = jnp.pad(b_out, (0, L - k)).reshape(1, L)]
    squeeze x1, local copies, waits for them, and re-layouts: 0.51 us -> 1.19 us  [on_device(): ogb[1, :k]]
    squeeze x1, local copies, waits for them, and re-layouts: 0.51 us -> 1.18 us  [on_device(): ogb[0]]
where the time goes in v4:
time: 62.3 us; the launch traced here: 62 us
  Pallas kernels  52.7 us (85%)
  local copies, waits for them, and re-layouts  8.62 us (14%)
  between operations  0.65 us (1%)
    pallas_call x1, Pallas kernels, on_device(): pl.pallas_call(functools.partial(kernel, cfg), out_shape=(jax.ShapeDtypeS...  52.7 us
    unnamed x13, local copies, waits for them, and re-layouts  5.09 us

profile of v4, /device:TPU:0, one launch (start us, length us, event | category | flops | bytes accessed | tf_op | source)
XLA Modules:
  0.0 62.0 jit_solution(12465760938117010073)
XLA Ops:
  0.6 1.2 %pad_bitcast_fusion.bo_ref = f32[1,128]{1,0:T(1,128)} fusion(f32[18]{0:T(128)} %param.15), kind=kLoop, calls=%fused_computation.2 | loop fusion | bytes 584 | tf_op jit(solution)/shard_map/reshape | solution.py:277
  1.8 52.7 %shard_map.135 = (f32[16,64,128]{2,1,0:T(8,128)}, f32[256,64]{1,0:T(8,128)}, f32[16,32,128]{2,1,0:T(8,128)}, f32[128,128]{1,0:T(8,128)}, f32[18,128]{1,0:T(8,128)}, /*index=5*/f32[8,128]{1,0:T(8,128)}) custom-call(bf16[16,64,128]{2,1,0:T(8,128)(2,1)} %top_ref.1, bf16[256,64]{1,0:T(8,128)(2,1)} %bitcast.16, bf16[16,32,128]{2,1,0:T(8,128)(2,1)} %bitcast.14, ...), custom_call_target="tpu_custom_call" | custom-call | tf_op jit(solution)/shard_map/pallas_call | solution.py:285
  54.5 1.2 %slice_bitcast_fusion = f32[18]{0:T(128)} fusion(f32[8,128]{1,0:T(8,128)} %get-tuple-element.17), kind=kLoop, calls=%fused_computation | loop fusion | bytes 144 | tf_op jit(solution)/shard_map/squeeze | solution.py:318
  55.7 1.2 %slice_bitcast_fusion.1 = f32[128]{0:T(128)} fusion(f32[8,128]{1,0:T(8,128)} %get-tuple-element.17), kind=kLoop, calls=%fused_computation.1 | loop fusion | bytes 1024 | tf_op jit(solution)/shard_map/squeeze | solution.py:318
  56.9 0.0 copy-start.1
  56.9 1.9 %copy.20 = f32[16,64,128]{2,1,0:T(8,128)} copy(f32[16,64,128]{2,1,0:T(8,128)} %get-tuple-element.26) | data formatting | bytes 1048576
  58.8 0.0 copy-done.1
  58.8 0.0 copy-start
  58.8 0.7 %copy.21 = f32[16,16,64]{2,1,0:T(8,128)} copy(f32[16,16,64]{2,1,0:T(8,128)S(1)} %bitcast.15) | data formatting | bytes 131072
  59.4 0.3 copy-done
  59.8 0.0 copy-start.2
  59.8 0.7 %copy.22 = f32[128,16,32]{0,2,1:T(8,128)} copy(f32[128,16,32]{0,2,1:T(8,128)S(1)} %bitcast.13) | data formatting | bytes 524288
  60.5 0.2 copy-done.2
  60.7 0.0 copy-start.3
  60.7 0.6 %copy.23 = f32[128,128]{1,0:T(8,128)} copy(f32[128,128]{1,0:T(8,128)S(1)} %copy-done.2) | data formatting | bytes 131072
  61.3 0.1 copy-done.3
  61.4 0.6 copy.24
Async XLA Ops:
  56.9 1.9 %copy-start.1 = (f32[256,64]{1,0:T(8,128)S(1)}, f32[256,64]{1,0:T(8,128)}, u32[]{:S(2)}) copy-start(f32[256,64]{1,0:T(8,128)} %get-tuple-element.14) | copy-start | bytes 196612
  58.8 1.0 %copy-start = (f32[16,32,128]{2,1,0:T(8,128)S(1)}, f32[16,32,128]{2,1,0:T(8,128)}, u32[]{:S(2)}) copy-start(f32[16,32,128]{2,1,0:T(8,128)} %get-tuple-element.15) | copy-start | bytes 786436
  59.8 0.9 %copy-start.2 = (f32[128,128]{1,0:T(8,128)S(1)}, f32[128,128]{1,0:T(8,128)}, u32[]{:S(2)}) copy-start(f32[128,128]{1,0:T(8,128)} %get-tuple-element.29) | copy-start | bytes 196612
  60.7 0.7 %copy-start.3 = (f32[18,128]{1,0:T(8,128)S(1)}, f32[18,128]{1,0:T(8,128)}, u32[]{:S(2)}) copy-start(f32[18,128]{1,0:T(8,128)} %get-tuple-element.18) | copy-start | bytes 27652
